TPU v7x, 32 devices: a whole 2x2x4 slice. The times are simulated.
32 devices in a mesh: parts: 2 (over x), tile: 16 (over z, y, core).
Axes of the slice: x: 2, y: 2, z: 4, core: 2. Of those that a mesh axis runs over, the one named last changes fastest.
Arguments:
- probe_wave: float32 [2, 128, 128], replicated, may hold values from -6 to 6
- object_slices: float32 [8, 2, 2048, 1024], P('parts', None, 'tile'), parts along dimension 0, may hold values from -4 to 4
- intensities: float32 [256, 128, 128], P(('parts', 'tile')), parts along dimension 0, may hold values from 0 to 2
- row_offset: int32 [256], P(('parts', 'tile')), parts along dimension 0, may hold values from 0 to 127
- col_offset: int32 [256], P(('parts', 'tile')), parts along dimension 0, may hold values from 0 to 896
- counts: int32 [32], P(('parts', 'tile')), parts along dimension 0, may hold values from 1 to 8, 64 in all
Outputs:
- object_grad: float32 [8, 2, 2048, 1024], P('parts', None, 'tile'), parts along dimension 0
- misfit_total: float32 [2], P('parts'), parts along dimension 0
There are 2 independent parts, one for each index of `parts`. A program takes and returns all parts, laid end to end along the dimension named above; an argument that names none is the same for every part. Nothing has to cross between parts.
Inputs may be any that keep to these rules, and one draw needn't show every extreme that they name: `counts`: every strip holds at least one position; some strip holds exactly 8.
All inputs are finite; a program needn't handle non-finite values. No bound on the sum of `counts` on one device may be relied on, other than what follows from the above.
Results may differ from a plain program's by a relative error of at most 0.0003.
Values sent between devices are 32-bit elements; how exact they have to be, the bound alone decides.
No kernel may reach another device: no remote copies, remote signals or barrier semaphores. Data moves between devices by JAX's collectives and lax.ppermute only.
A program may use at most 128 MiB of HBM per device.

v0:
```python
import functools

import jax
import jax.numpy as jnp
import ml_dtypes
import numpy as np
from jax import lax
from jax.experimental import pallas as pl
from jax.experimental.pallas import tpu as pltpu
from jax.sharding import PartitionSpec as P

BATCH = 4
UNIT = 8
ROW, COL, AT_PUSH, AT_BACK, AT_PULL, PUSHED, KEPT, TOTALS = range(8)


def make_tables(width):
    indices = np.arange(width)
    dft = np.exp(-2j * np.pi * (np.outer(indices, indices) % width) / width) / np.sqrt(width)
    freqs = np.where(indices < width // 2, indices, indices - width).astype(np.float64)
    along = np.conj(dft) @ (np.exp(-0.0015j * freqs**2)[:, None] * dft)
    out = []
    for matrix in (along, dft):
        left = np.block([[matrix.real, -matrix.imag], [matrix.imag, matrix.real]])
        forms = []
        for form in (left, left.T):
            form = form.astype(np.float32)
            high = form.astype(ml_dtypes.bfloat16)
            low = (form - high.astype(np.float32)).astype(ml_dtypes.bfloat16)
            forms.append(np.stack([high, low]))
        out.append(np.stack(forms))
    return np.stack(out)


def split(x):
    high = x.astype(jnp.bfloat16)
    return high, (x - high.astype(jnp.float32)).astype(jnp.bfloat16)


def dot(a, b):
    return jnp.dot(a, b, preferred_element_type=jnp.float32)


def one_sided(tables, which, form, re, im):
    width = re.shape[0]
    high, low = split(jnp.concatenate([re, im], axis=1))
    m_high, m_low = tables[which, form, 0], tables[which, form, 1]
    out = dot(high, m_high) + (dot(high, m_low) + dot(low, m_high))
    return out[:, :width], out[:, width:]


def two_sided(tables, which, conj, re, im):
    form = 0 if conj else 1
    half = [one_sided(tables, which, form, a, b) for a, b in zip(re, im)]
    full = [one_sided(tables, which, form, a.T, b.T) for a, b in half]
    return [a.T for a, _ in full], [b.T for _, b in full]


def field_grads(tables, wave_ref, window_ref, measured, scales):
    batch, slices = wave_ref.shape[:2]
    for layer in range(slices):
        re, im = [], []
        for b in range(batch):
            w_re, w_im = wave_ref[b, layer, 0], wave_ref[b, layer, 1]
            t_re, t_im = window_ref[b, layer, 0], window_ref[b, layer, 1]
            re.append(w_re * t_re - w_im * t_im)
            im.append(w_re * t_im + w_im * t_re)
        if layer + 1 < slices:
            re, im = two_sided(tables, 0, False, re, im)
            for b in range(batch):
                wave_ref[b, layer + 1, 0] = re[b]
                wave_ref[b, layer + 1, 1] = im[b]
    re, im = two_sided(tables, 1, False, re, im)
    loss = 0.0
    back_re, back_im = [], []
    for b in range(batch):
        misfit = re[b] * re[b] + im[b] * im[b] - measured[b]
        loss = loss + scales[b] * (0.25 * jnp.sum(misfit * misfit))
        back_re.append(misfit * re[b])
        back_im.append(misfit * im[b])
    re, im = two_sided(tables, 1, True, back_re, back_im)
    for layer in reversed(range(slices)):
        upper_re, upper_im = [], []
        for b in range(batch):
            w_re, w_im = wave_ref[b, layer, 0], wave_ref[b, layer, 1]
            t_re, t_im = window_ref[b, layer, 0], window_ref[b, layer, 1]
            window_ref[b, layer, 0] = re[b] * w_re + im[b] * w_im
            window_ref[b, layer, 1] = im[b] * w_re - re[b] * w_im
            upper_re.append(re[b] * t_re + im[b] * t_im)
            upper_im.append(im[b] * t_re - re[b] * t_im)
        if layer > 0:
            re, im = two_sided(tables, 0, True, upper_re, upper_im)
    return loss


def place(plan_ref, slot, width, columns):
    row, col = plan_ref[ROW, slot], plan_ref[COL, slot]
    tile = col // width
    here = pl.ds(pl.multiple_of(tile * width, width), width)
    after = jnp.minimum(tile + 1, columns // width - 1)
    there = pl.ds(pl.multiple_of(after * width, width), width)
    return row, col - tile * width, here, there


def sizes(cap, width):
    whole = cap * width // UNIT
    return whole * 5 // 16, whole // 4, whole * 5 // 16


def make_plan(meta_ref, plan_ref, width, room):
    cap = plan_ref.shape[1]
    units = width // UNIT
    seen_units = width // (UNIT * UNIT)
    shape = (UNIT, 128)
    choice = lax.broadcasted_iota(jnp.int32, shape, 0) * 128 + lax.broadcasted_iota(jnp.int32, shape, 1)
    zero = jnp.zeros(shape, jnp.int32)
    push, back, pull, kept, bad = zero, zero, zero, zero, (choice >= (1 << cap)).astype(jnp.int32)
    count = meta_ref[0]
    for s in range(cap):
        row = meta_ref[1 + s]
        crosses = jnp.logical_and(s < count, row > 0).astype(jnp.int32)
        taken = (choice >> s) & 1
        ahead = units - row // UNIT
        push += taken * (ahead + seen_units)
        back += taken * ahead
        pull += (1 - taken) * (crosses * ((row + UNIT - 1) // UNIT))
        kept += 1 - taken
        bad += taken * (1 - crosses)
    bad += (push > room[0]).astype(jnp.int32) + (back > room[1]).astype(jnp.int32) + (pull > room[2]).astype(jnp.int32)
    score = (kept + 16 * (bad > 0).astype(jnp.int32)) * (1 << cap) + choice
    best = jnp.min(score.astype(jnp.float32)).astype(jnp.int32)
    at_push = at_back = at_pull = n_pushed = n_kept = jnp.int32(0)
    for s in range(cap):
        plan_ref[PUSHED, s] = 0
        plan_ref[KEPT, s] = 0
        plan_ref[TOTALS, s] = 0
    for s in range(cap):
        row = meta_ref[1 + s]
        taken = (best >> s) & 1
        kept = jnp.where(s < count, 1 - taken, 0)
        plan_ref[ROW, s] = row
        plan_ref[COL, s] = meta_ref[1 + cap + s]
        plan_ref[AT_PUSH, s] = at_push
        plan_ref[AT_BACK, s] = at_back
        plan_ref[AT_PULL, s] = at_pull

        @pl.when(taken > 0)
        def _():
            plan_ref[PUSHED, n_pushed] = s

        @pl.when(kept > 0)
        def _():
            plan_ref[KEPT, n_kept] = s

        ahead = units - row // UNIT
        at_push += taken * (ahead + seen_units)
        at_back += taken * ahead
        at_pull += kept * ((row + UNIT - 1) // UNIT)
        n_pushed += taken
        n_kept += kept
    plan_ref[TOTALS, 0] = n_pushed
    plan_ref[TOTALS, 1] = n_kept


def pack(plan_ref, slot, own_ref, buffer_ref, start, first_unit, last_unit):
    slices, planes, width, columns = own_ref.shape
    _, shift, here, there = place(plan_ref, slot, width, columns)
    first = lax.broadcasted_iota(jnp.int32, (UNIT, width), 1) >= shift

    def step(u, carry):
        rows = pl.ds(pl.multiple_of(u * UNIT, UNIT), UNIT)
        for l in range(slices):
            for p in range(planes):
                buffer_ref[start + u - first_unit, l * planes + p] = jnp.where(
                    first, own_ref[l, p, rows, here], own_ref[l, p, rows, there]
                )
        return carry

    lax.fori_loop(first_unit, last_unit, step, 0)


def push_kernel(meta_ref, own_hbm, seen_hbm, plan_ref, push_ref, own_ref, sem, sems, *, room):
    width = own_ref.shape[2]
    units, seen_units = width // UNIT, seen_hbm.shape[1]
    load = pltpu.make_async_copy(own_hbm, own_ref, sem)
    load.start()
    make_plan(meta_ref, plan_ref, width, room)

    def seen(i):
        slot = plan_ref[PUSHED, i]
        start = plan_ref[AT_PUSH, slot] + units - plan_ref[ROW, slot] // UNIT
        return pltpu.make_async_copy(seen_hbm.at[slot], push_ref.at[pl.ds(start, seen_units)], sems.at[i])

    def begin(i, carry):
        seen(i).start()
        return carry

    def step(i, carry):
        slot = plan_ref[PUSHED, i]
        pack(plan_ref, slot, own_ref, push_ref, plan_ref[AT_PUSH, slot], plan_ref[ROW, slot] // UNIT, units)
        return carry

    def end(i, carry):
        seen(i).wait()
        return carry

    lax.fori_loop(0, plan_ref[TOTALS, 0], begin, 0)
    shape = (UNIT, width)
    index = lax.broadcasted_iota(jnp.int32, shape, 0) * width + lax.broadcasted_iota(jnp.int32, shape, 1)
    told = jnp.zeros(shape, jnp.float32)
    for r in range(plan_ref.shape[0]):
        for s in range(plan_ref.shape[1]):
            told = jnp.where(index == r * width + s, plan_ref[r, s].astype(jnp.float32), told)
    push_ref[room[0], 0] = told
    load.wait()
    lax.fori_loop(0, plan_ref[TOTALS, 0], step, 0)
    lax.fori_loop(0, plan_ref[TOTALS, 0], end, 0)


def pull_kernel(told_ref, own_ref, plan_ref, pull_ref, whole_ref, numbers_ref, sem):
    whole_ref[...] = told_ref[told_ref.shape[0] - 1, 0].astype(jnp.int32)
    copy = pltpu.make_async_copy(whole_ref, numbers_ref, sem)
    copy.start()
    copy.wait()
    for r in range(plan_ref.shape[0]):
        for s in range(plan_ref.shape[1]):
            plan_ref[r, s] = numbers_ref[r, s]

    def step(i, carry):
        slot = plan_ref[KEPT, i]
        end = (plan_ref[ROW, slot] + UNIT - 1) // UNIT
        pack(plan_ref, slot, own_ref, pull_ref, plan_ref[AT_PULL, slot], 0, end)
        return carry

    lax.fori_loop(0, plan_ref[TOTALS, 1], step, 0)


def grad_kernel(plan_ref, probe_ref, own_ref, came_ref, tables_ref, *refs, pushed):
    if pushed:
        grad_ref, back_ref, loss_ref, wave_ref, window_ref = refs
    else:
        loss_in_ref, seen_ref, _, grad_ref, back_ref, loss_ref, wave_ref, window_ref = refs
    slices, planes, width, columns = own_ref.shape
    units = width // UNIT
    seen_units = width // (UNIT * UNIT)
    last = came_ref.shape[0] - 1
    if pushed:
        grad_ref[...] = jnp.zeros_like(grad_ref)
    row_iota = lax.broadcasted_iota(jnp.int32, (width, width), 0)
    lane_iota = lax.broadcasted_iota(jnp.int32, (width, width), 1)
    count = plan_ref[TOTALS, 0 if pushed else 1]

    def step(group, loss):
        slots, scales, measured = [], [], []
        for b in range(BATCH):
            live = group * BATCH + b < count
            slot = plan_ref[PUSHED if pushed else KEPT, jnp.where(live, group * BATCH + b, group * BATCH)]
            slots.append(slot)
            scales.append(live.astype(jnp.float32))
            row, shift, here, there = place(plan_ref, slot, width, columns)
            mine = row_iota < row if pushed else row_iota >= row
            first = lane_iota >= shift
            if pushed:
                start = plan_ref[AT_PUSH, slot] - row // UNIT
                seen = came_ref[pl.ds(jnp.minimum(start + units, last + 1 - seen_units), seen_units)]
                measured.append(seen.reshape(width, width))
            else:
                start = plan_ref[AT_PULL, slot]
                measured.append(seen_ref[slot])
            at = [jnp.clip(start + u, 0, last) for u in range(units)]
            for l in range(slices):
                for p in range(planes):
                    theirs = jnp.concatenate([came_ref[i, l * planes + p] for i in at], axis=0)
                    ours = jnp.where(first, own_ref[l, p, :, here], own_ref[l, p, :, there])
                    window_ref[b, l, p] = jnp.where(mine, ours, theirs)
            for p in range(planes):
                wave_ref[b, 0, p] = pltpu.roll(pltpu.roll(probe_ref[p], row, 0), shift, 1)
        loss = loss + field_grads(tables_ref, wave_ref, window_ref, measured, scales)
        for b in range(BATCH):
            row, shift, here, there = place(plan_ref, slots[b], width, columns)
            mine = row_iota < row if pushed else row_iota >= row
            first = lane_iota >= shift
            if pushed:
                start, begin, end = plan_ref[AT_BACK, slots[b]], row // UNIT, units
            else:
                start, begin, end = plan_ref[AT_PULL, slots[b]], 0, (row + UNIT - 1) // UNIT

            @pl.when(scales[b] > 0)
            def _(b=b, mine=mine, first=first, here=here, there=there, start=start, begin=begin, end=end):
                for l in range(slices):
                    for p in range(planes):
                        ours = jnp.where(mine, window_ref[b, l, p], 0.0)
                        grad_ref[l, p, :, here] += jnp.where(first, ours, 0.0)
                        grad_ref[l, p, :, there] += jnp.where(first, 0.0, ours)

                def unit(u, carry):
                    rows = pl.ds(pl.multiple_of(u * UNIT, UNIT), UNIT)
                    for l in range(slices):
                        for p in range(planes):
                            back_ref[start + u - begin, l * planes + p] = window_ref[b, l, p, rows, :]
                    return carry

                lax.fori_loop(begin, end, unit, 0)

        return loss

    before = jnp.float32(0.0) if pushed else loss_in_ref[0]
    loss_ref[0] = lax.fori_loop(0, (count + BATCH - 1) // BATCH, step, before)


def after_kernel(x_ref, *refs):
    pass


def add(plan, slot, grad_ref, layers, came, start, begin, end, below):
    planes, width, columns = grad_ref.shape[1:]
    row, shift, here, there = place(plan, slot, width, columns)
    first = lax.broadcasted_iota(jnp.int32, (UNIT, width), 1) >= shift
    row_iota = lax.broadcasted_iota(jnp.int32, (UNIT, width), 0)

    def unit(u, carry):
        rows = pl.ds(pl.multiple_of(u * UNIT, UNIT), UNIT)
        at = u * UNIT + row_iota
        mine = at < row if below else at >= row
        for l in layers:
            for p in range(planes):
                piece = jnp.where(mine, came[start + u - begin, l * planes + p], 0.0)
                grad_ref[l, p, rows, here] += jnp.where(first, piece, 0.0)
                grad_ref[l, p, rows, there] += jnp.where(first, 0.0, piece)
        return carry

    lax.fori_loop(begin, end, unit, 0)


def add_returned_kernel(plan_ref, returned_ref, grad_in_ref, grad_ref):
    slices, _, width, _ = grad_ref.shape

    def step(i, carry):
        slot = plan_ref[PUSHED, i]
        at, low = plan_ref[AT_BACK, slot], plan_ref[ROW, slot] // UNIT
        add(plan_ref, slot, grad_ref, range(slices), returned_ref, at, low, width // UNIT, False)
        return carry

    lax.fori_loop(0, plan_ref[TOTALS, 0], step, 0)


def add_given_kernel(before_ref, given_ref, grad_ref, grad_hbm, sems):
    slices = grad_ref.shape[0]
    stores = [pltpu.make_async_copy(grad_ref.at[l], grad_hbm.at[l], sems.at[l]) for l in range(slices)]
    for l in range(slices):

        def step(i, carry, l=l):
            slot = before_ref[KEPT, i]
            end = (before_ref[ROW, slot] + UNIT - 1) // UNIT
            add(before_ref, slot, grad_ref, [l], given_ref, before_ref[AT_PULL, slot], 0, end, True)
            return carry

        lax.fori_loop(0, before_ref[TOTALS, 1], step, 0)
        stores[l].start()
    for store in stores:
        store.wait()


def shifted(x, axis, by):
    peers = lax.axis_size(axis)
    return lax.ppermute(x, axis, [(i, (i + by) % peers) for i in range(peers)])


def total_stages(peers):
    stages, step = [], 1
    while step < peers:
        radix = 4 if step * 4 <= peers else 2
        stages.append((step, radix))
        step *= radix
    return stages


def partial_total(x, axis, stage):
    peers = lax.axis_size(axis)
    step, radix = stage

    def other(by):
        return lax.ppermute(x, axis, [(i, i ^ by) for i in range(peers)])

    if radix == 2:
        return x + other(step)
    return (x + other(step)) + (other(2 * step) + other(3 * step))


def local(probe_wave, object_slices, intensities, row_offset, col_offset, counts):
    width = probe_wave.shape[-1]
    slices, planes = object_slices.shape[:2]
    cap = row_offset.shape[0]
    units = width // UNIT
    seen_units = width // (UNIT * UNIT)
    tables = jnp.asarray(make_tables(width))
    seen = intensities.reshape(cap, seen_units, UNIT, UNIT, width)
    room = sizes(cap, width)
    smem = pl.BlockSpec(memory_space=pltpu.SMEM)
    vmem = pl.BlockSpec(memory_space=pltpu.VMEM)
    hbm = pl.BlockSpec(memory_space=pltpu.HBM)
    anywhere = pl.BlockSpec(memory_space=pl.ANY)
    f32 = jnp.float32

    def packed(n):
        return (n, slices * planes, UNIT, width)

    def shape(dims, dtype=f32):
        return jax.ShapeDtypeStruct(dims, dtype)

    def params(mib):
        return pltpu.CompilerParams(vmem_limit_bytes=int(mib * 2**20))

    def cost(us):
        return pl.CostEstimate(flops=int(us * 1e9), bytes_accessed=int(us * 1e6), transcendentals=0)

    strip = object_slices.shape
    meta = jnp.concatenate([counts, row_offset, col_offset])
    plan_shape = shape((8, cap), jnp.int32)
    plan, push, own = pl.pallas_call(
        functools.partial(push_kernel, room=room),
        out_shape=(plan_shape, shape(packed(room[0] + 1)), shape(strip)),
        in_specs=[smem, hbm, hbm],
        out_specs=(smem, vmem, vmem),
        scratch_shapes=[pltpu.SemaphoreType.DMA, pltpu.SemaphoreType.DMA((cap,))],
        compiler_params=params(48),
        cost_estimate=cost(4),
        name="pack_pushed",
    )(meta, object_slices, seen)
    pushed = shifted(push, "tile", 1)
    before, pull = pl.pallas_call(
        pull_kernel,
        out_shape=(plan_shape, shape(packed(room[2]))),
        in_specs=[vmem, vmem],
        out_specs=(smem, vmem),
        scratch_shapes=[
            pltpu.VMEM((UNIT, width), jnp.int32),
            pltpu.SMEM((UNIT, width), jnp.int32),
            pltpu.SemaphoreType.DMA,
        ],
        compiler_params=params(16),
        cost_estimate=cost(2),
        name="pack_pulled",
    )(pushed, own)
    pulled = shifted(pull, "tile", -1)

    def grads(plan, came, back, *kept):
        return pl.pallas_call(
            functools.partial(grad_kernel, pushed=not kept),
            out_shape=(shape(strip), shape(packed(back)), shape((1,))),
            in_specs=[smem] + [vmem] * 4 + ([smem, vmem, vmem] if kept else []),
            out_specs=(vmem, vmem, smem),
            scratch_shapes=[
                pltpu.VMEM((BATCH, slices, planes, width, width), f32),
                pltpu.VMEM((BATCH, slices, planes, width, width), f32),
            ],
            input_output_aliases={7: 0} if kept else {},
            compiler_params=params(24),
            cost_estimate=cost(10),
            name="grads_kept" if kept else "grads_pushed",
        )(plan, probe_wave, own, came, tables, *kept)

    grad, back, loss = grads(before, pushed, room[1])
    returned = shifted(back, "tile", -1)
    grad, back, loss = grads(plan, pulled, room[2], loss, intensities, grad)
    stages = total_stages(lax.axis_size("tile"))
    loss = partial_total(loss, "tile", stages[0])
    back = pl.pallas_call(
        after_kernel,
        out_shape=shape(back.shape),
        in_specs=[anywhere] * 3,
        out_specs=anywhere,
        input_output_aliases={0: 0},
        compiler_params=params(4),
        name="after_returned",
    )(back, returned, loss)
    given = shifted(back, "tile", 1)
    for stage in stages[1:]:
        loss = partial_total(loss, "tile", stage)
    misfit_total = loss.reshape(1)
    grad = pl.pallas_call(
        add_returned_kernel,
        out_shape=shape(strip),
        in_specs=[smem, vmem, vmem],
        out_specs=vmem,
        input_output_aliases={2: 0},
        compiler_params=params(4),
        cost_estimate=cost(1),
        name="add_returned",
    )(plan, returned, grad)
    grad = pl.pallas_call(
        add_given_kernel,
        out_shape=shape(strip),
        in_specs=[smem, vmem, vmem],
        out_specs=hbm,
        scratch_shapes=[pltpu.SemaphoreType.DMA((slices,))],
        compiler_params=params(4),
        cost_estimate=cost(4),
        name="add_given",
    )(before, given, grad)
    return (grad, misfit_total)


def solution(mesh):
    placed = (
        P(),
        P("parts", None, "tile", None),
        P(("parts", "tile"), None, None),
        P(("parts", "tile")),
        P(("parts", "tile")),
        P(("parts", "tile")),
    )
    return jax.shard_map(
        local,
        mesh=mesh,
        in_specs=placed,
        out_specs=(P("parts", None, "tile", None), P("parts")),
        check_vma=False,
    )
```

profile of v0, /device:TPU:0, one launch (start us, length us, event | category | flops | bytes accessed | tf_op | source)
XLA Modules:
  0.0 85.7 jit_solution(5843853414654347932)
XLA Ops:
  1.3 0.7 pad_add_fusion.meta_ref
  2.0 0.0 copy-start
  2.0 1.0 %copy-done = f32[8,128,128]{2,1,0:T(8,128)S(1)} copy-done((f32[8,128,128]{2,1,0:T(8,128)S(1)}, f32[8,128,128]{2,1,0:T(8,128)}, u32[]{:S(2)}) %copy-start) | copy-done | bytes 524312
  3.1 4.1 %pack_pushed.1 = (s32[8,8]{1,0:T(8,128)S(1)}, f32[41,8,8,128]{3,2,1,0:T(8,128)S(1)}, f32[4,2,128,1024]{3,2,1,0:T(8,128)S(1)}) custom-call(s32[17]{0:T(128)S(1)} %pad_add_fusion.meta_ref, f32[4,2,128,1024]{3,2,1,0:T(8,128)} %own_hbm.1, f32[8,2,8,8,128]{4,3,2,1,0:T(8,128)S(1)} %bitcast.1), custom_call_target="tpu_custom_call" | custom-call | flops 4000000000 | bytes 4000000 | tf_op jit(solution)/shard_map/pack_pushed/pallas_call | solution.py:420
  7.2 0.4 collective-permute-start
  7.6 20.4 %collective-permute-done.told_ref.came_ref = f32[41,8,8,128]{3,2,1,0:T(8,128)S(1)} collective-permute-done((f32[41,8,8,128]{3,2,1,0:T(8,128)S(1)}, f32[41,8,8,128]{3,2,1,0:T(8,128)S(1)}, u32[]{:S(2)}, u32[]{:S(2)}) %collective-permute-start) | collective-permute-done | bytes 1343520 | tf_op jit(solution)/shard_map/ppermute | solution.py:366
  28.0 0.0 copy-start.1
  28.0 0.0 copy-start.2
  28.0 1.3 %pack_pulled.1 = (s32[8,8]{1,0:T(8,128)S(1)}, f32[40,8,8,128]{3,2,1,0:T(8,128)S(1)}) custom-call(f32[41,8,8,128]{3,2,1,0:T(8,128)S(1)} %collective-permute-done.told_ref.came_ref, f32[4,2,128,1024]{3,2,1,0:T(8,128)S(1)} %get-tuple-element.14.own_ref), custom_call_target="tpu_custom_call" | custom-call | flops 2000000000 | bytes 2000000 | tf_op jit(solution)/shard_map/pack_pulled/pallas_call | solution.py:431
  29.3 0.1 collective-permute-start.1
  29.4 0.0 copy-done.1
  29.4 0.0 copy-done.2
  29.4 8.2 %grads_pushed.1 = (f32[4,2,128,1024]{3,2,1,0:T(8,128)S(1)}, f32[32,8,8,128]{3,2,1,0:T(8,128)S(1)}, f32[1]{0:T(128)}) custom-call(s32[8,8]{1,0:T(8,128)S(1)} %get-tuple-element.15.plan_ref.before_ref, f32[2,128,128]{2,1,0:T(8,128)S(1)} %copy-done.1, f32[4,2,128,1024]{3,2,1,0:T(8,128)S(1)} %get-tuple-element.14.own_ref, ...), custom_call_target="tpu_custom_call" | custom-call | flops 10000000000 | bytes 10000000 | tf_op jit(solution)/shard_map/grads_pushed/pallas_call | solution.py:448
  37.6 9.8 %collective-permute-start.2 = (f32[32,8,8,128]{3,2,1,0:T(8,128)S(1)}, f32[32,8,8,128]{3,2,1,0:T(8,128)S(1)}, u32[]{:S(2)}, u32[]{:S(2)}) collective-permute-start(f32[32,8,8,128]{3,2,1,0:T(8,128)S(1)} %get-tuple-element.21), channel_id=1, source_target_pairs={{0,15},{1,0},{2,1},{3,2},{4,3},{5,4},{6,5},{7,6},{8,7},{9,8},{10,9... | collective-permute-start | bytes 3145736 | tf_op jit(solution)/shard_map/ppermute | solution.py:366
  47.4 0.0 collective-permute-done.1.came_ref
  47.4 9.3 %grads_kept.1 = (f32[4,2,128,1024]{3,2,1,0:T(8,128)S(1)}, f32[40,8,8,128]{3,2,1,0:T(8,128)S(1)}, f32[1]{0:T(128)}) custom-call(s32[8,8]{1,0:T(8,128)S(1)} %get-tuple-element.16.plan_ref, f32[2,128,128]{2,1,0:T(8,128)S(1)} %copy-done.1, f32[4,2,128,1024]{3,2,1,0:T(8,128)S(1)} %get-tuple-element.14.own_ref, ...), custom_call_target="tpu_custom_call", output_to_operand_aliasing={{0}: (7, {})} | custom-call | flops 10000000000 | bytes 10000000 | tf_op jit(solution)/shard_map/grads_kept/pallas_call | solution.py:448
  56.7 0.1 collective-permute-start.5
  56.7 0.1 collective-permute-start.4
  56.8 1.8 %collective-permute-start.3 = (f32[1]{0:T(128)}, f32[1]{0:T(128)}, u32[]{:S(2)}, u32[]{:S(2)}) collective-permute-start(f32[1]{0:T(128)} %get-tuple-element.22), channel_id=1, source_target_pairs={{0,1},{1,0},{2,3},{3,2},{4,5},{5,4},{6,7},{7,6},{8,9},{9,8},{10,11... | collective-permute-start | bytes 20 | tf_op jit(solution)/shard_map/ppermute | solution.py:383
  58.6 1.0 %collective-permute-done.3 = f32[1]{0:T(128)} collective-permute-done((f32[1]{0:T(128)}, f32[1]{0:T(128)}, u32[]{:S(2)}, u32[]{:S(2)}) %collective-permute-start.3) | collective-permute-done | bytes 36 | tf_op jit(solution)/shard_map/ppermute | solution.py:383
  60.9 0.0 collective-permute-done.5
  60.9 0.0 collective-permute-done.4
  62.1 0.0 collective-permute-done.2.refs_0_.returned_ref
  62.1 0.3 collective-permute-start.6
  62.4 1.9 %add_returned.1.grad_ref = f32[4,2,128,1024]{3,2,1,0:T(8,128)S(1)} custom-call(s32[8,8]{1,0:T(8,128)S(1)} %get-tuple-element.16.plan_ref, f32[32,8,8,128]{3,2,1,0:T(8,128)S(1)} %collective-permute-done.2.refs_0_.returned_ref, f32[4,2,128,1024]{3,2,1,0:T(8,128)S(1)} %get-tuple-element.23.grad_in_ref), custom_call_target="tpu_custom_call", output_to_operand_aliasing={{}: (2, {})} | custom-call | flops 1000000000 | bytes 1000000 | tf_op jit(solution)/shard_map/add_returned/pallas_call | solution.py:481
  64.4 1.4 %collective-permute-start.9 = (f32[1]{0:T(128)}, f32[1]{0:T(128)}, u32[]{:S(2)}, u32[]{:S(2)}) collective-permute-start(f32[1]{0:T(128)} %add.20.refs_1_), channel_id=1, source_target_pairs={{0,12},{1,13},{2,14},{3,15},{4,8},{5,9},{6,10},{7,11},{8,4},{9,5},... | collective-permute-start | bytes 20 | tf_op jit(solution)/shard_map/ppermute | solution.py:383
  65.7 1.4 %collective-permute-start.8 = (f32[1]{0:T(128)}, f32[1]{0:T(128)}, u32[]{:S(2)}, u32[]{:S(2)}) collective-permute-start(f32[1]{0:T(128)} %add.20.refs_1_), channel_id=1, source_target_pairs={{0,8},{1,9},{2,10},{3,11},{4,12},{5,13},{6,14},{7,15},{8,0},{9,1},... | collective-permute-start | bytes 20 | tf_op jit(solution)/shard_map/ppermute | solution.py:383
  67.1 5.6 %collective-permute-start.7 = (f32[1]{0:T(128)}, f32[1]{0:T(128)}, u32[]{:S(2)}, u32[]{:S(2)}) collective-permute-start(f32[1]{0:T(128)} %add.20.refs_1_), channel_id=1, source_target_pairs={{0,4},{1,5},{2,6},{3,7},{4,0},{5,1},{6,2},{7,3},{8,12},{9,13},{10,... | collective-permute-start | bytes 20 | tf_op jit(solution)/shard_map/ppermute | solution.py:383
  72.7 0.2 collective-permute-done.7
  73.6 0.0 collective-permute-done.9
  74.8 7.1 %collective-permute-done.6.given_ref = f32[40,8,8,128]{3,2,1,0:T(8,128)S(1)} collective-permute-done((f32[40,8,8,128]{3,2,1,0:T(8,128)S(1)}, f32[40,8,8,128]{3,2,1,0:T(8,128)S(1)}, u32[]{:S(2)}, u32[]{:S(2)}) %collective-permute-start.6) | collective-permute-done | bytes 1310752 | tf_op jit(solution)/shard_map/ppermute | solution.py:366
  81.9 2.6 %add_given.1 = f32[4,2,128,1024]{3,2,1,0:T(8,128)} custom-call(s32[8,8]{1,0:T(8,128)S(1)} %get-tuple-element.15.plan_ref.before_ref, f32[40,8,8,128]{3,2,1,0:T(8,128)S(1)} %collective-permute-done.6.given_ref, f32[4,2,128,1024]{3,2,1,0:T(8,128)S(1)} %add_returned.1.grad_ref), custom_call_target="tpu_custom_call" | custom-call | flops 4000000000 | bytes 4000000 | tf_op jit(solution)/shard_map/add_given/pallas_call | solution.py:491
  (2 shorter events, 0.0 us)
Async XLA Ops:
  2.0 1.0 %copy-start = (f32[8,128,128]{2,1,0:T(8,128)S(1)}, f32[8,128,128]{2,1,0:T(8,128)}, u32[]{:S(2)}) copy-start(f32[8,128,128]{2,1,0:T(8,128)} %refs_1_.1) | copy-start | bytes 1572868
  7.2 20.8 %collective-permute-start = (f32[41,8,8,128]{3,2,1,0:T(8,128)S(1)}, f32[41,8,8,128]{3,2,1,0:T(8,128)S(1)}, u32[]{:S(2)}, u32[]{:S(2)}) collective-permute-start(f32[41,8,8,128]{3,2,1,0:T(8,128)S(1)} %get-tuple-element.13), channel_id=1, source_target_pairs={{0,1},{1,2},{2,3},{3,4},{4,5},{5,6},{6,7},{7,8},{8,9},{9,10},{10,1... | collective-permute-start | bytes 4030472 | tf_op jit(solution)/shard_map/ppermute | solution.py:366
  28.0 1.4 %copy-start.1 = (f32[2,128,128]{2,1,0:T(8,128)S(1)}, f32[2,128,128]{2,1,0:T(8,128)}, u32[]{:S(2)}) copy-start(f32[2,128,128]{2,1,0:T(8,128)} %probe_ref.3) | copy-start | bytes 393220
  28.0 1.4 %copy-start.2 = (bf16[2,2,2,256,256]{4,3,2,1,0:T(8,128)(2,1)S(1)}, bf16[2,2,2,256,256]{4,3,2,1,0:T(8,128)(2,1)}, u32[]{:S(2)}) copy-start(bf16[2,2,2,256,256]{4,3,2,1,0:T(8,128)(2,1)} %constant.2.clone.tables_ref) | copy-start | bytes 3145732
  29.3 18.1 %collective-permute-start.1 = (f32[40,8,8,128]{3,2,1,0:T(8,128)S(1)}, f32[40,8,8,128]{3,2,1,0:T(8,128)S(1)}, u32[]{:S(2)}, u32[]{:S(2)}) collective-permute-start(f32[40,8,8,128]{3,2,1,0:T(8,128)S(1)} %get-tuple-element.17), channel_id=1, source_target_pairs={{0,15},{1,0},{2,1},{3,2},{4,3},{5,4},{6,5},{7,6},{8,7},{9,8},{10,9... | collective-permute-start | bytes 3932168 | tf_op jit(solution)/shard_map/ppermute | solution.py:366
  37.6 24.5 %collective-permute-start.2 = (f32[32,8,8,128]{3,2,1,0:T(8,128)S(1)}, f32[32,8,8,128]{3,2,1,0:T(8,128)S(1)}, u32[]{:S(2)}, u32[]{:S(2)}) collective-permute-start(f32[32,8,8,128]{3,2,1,0:T(8,128)S(1)} %get-tuple-element.21), channel_id=1, source_target_pairs={{0,15},{1,0},{2,1},{3,2},{4,3},{5,4},{6,5},{7,6},{8,7},{9,8},{10,9... | collective-permute-start | bytes 3145736 | tf_op jit(solution)/shard_map/ppermute | solution.py:366
  56.7 4.2 %collective-permute-start.5 = (f32[1]{0:T(128)}, f32[1]{0:T(128)}, u32[]{:S(2)}, u32[]{:S(2)}) collective-permute-start(f32[1]{0:T(128)} %get-tuple-element.22), channel_id=1, source_target_pairs={{0,3},{1,2},{2,1},{3,0},{4,7},{5,6},{6,5},{7,4},{8,11},{9,10},{10,... | collective-permute-start | bytes 20 | tf_op jit(solution)/shard_map/ppermute | solution.py:383
  56.7 4.2 %collective-permute-start.4 = (f32[1]{0:T(128)}, f32[1]{0:T(128)}, u32[]{:S(2)}, u32[]{:S(2)}) collective-permute-start(f32[1]{0:T(128)} %get-tuple-element.22), channel_id=1, source_target_pairs={{0,2},{1,3},{2,0},{3,1},{4,6},{5,7},{6,4},{7,5},{8,10},{9,11},{10,... | collective-permute-start | bytes 20 | tf_op jit(solution)/shard_map/ppermute | solution.py:383
  56.8 2.7 %collective-permute-start.3 = (f32[1]{0:T(128)}, f32[1]{0:T(128)}, u32[]{:S(2)}, u32[]{:S(2)}) collective-permute-start(f32[1]{0:T(128)} %get-tuple-element.22), channel_id=1, source_target_pairs={{0,1},{1,0},{2,3},{3,2},{4,5},{5,4},{6,7},{7,6},{8,9},{9,8},{10,11... | collective-permute-start | bytes 20 | tf_op jit(solution)/shard_map/ppermute | solution.py:383
  62.1 19.8 %collective-permute-start.6 = (f32[40,8,8,128]{3,2,1,0:T(8,128)S(1)}, f32[40,8,8,128]{3,2,1,0:T(8,128)S(1)}, u32[]{:S(2)}, u32[]{:S(2)}) collective-permute-start(f32[40,8,8,128]{3,2,1,0:T(8,128)S(1)} %after_returned.1), channel_id=1, source_target_pairs={{0,1},{1,2},{2,3},{3,4},{4,5},{5,6},{6,7},{7,8},{8,9},{9,10},{10,1... | collective-permute-start | bytes 3932168 | tf_op jit(solution)/shard_map/ppermute | solution.py:366
  64.4 9.2 %collective-permute-start.9 = (f32[1]{0:T(128)}, f32[1]{0:T(128)}, u32[]{:S(2)}, u32[]{:S(2)}) collective-permute-start(f32[1]{0:T(128)} %add.20.refs_1_), channel_id=1, source_target_pairs={{0,12},{1,13},{2,14},{3,15},{4,8},{5,9},{6,10},{7,11},{8,4},{9,5},... | collective-permute-start | bytes 20 | tf_op jit(solution)/shard_map/ppermute | solution.py:383
  65.7 7.9 %collective-permute-start.8 = (f32[1]{0:T(128)}, f32[1]{0:T(128)}, u32[]{:S(2)}, u32[]{:S(2)}) collective-permute-start(f32[1]{0:T(128)} %add.20.refs_1_), channel_id=1, source_target_pairs={{0,8},{1,9},{2,10},{3,11},{4,12},{5,13},{6,14},{7,15},{8,0},{9,1},... | collective-permute-start | bytes 20 | tf_op jit(solution)/shard_map/ppermute | solution.py:383
  67.1 5.8 %collective-permute-start.7 = (f32[1]{0:T(128)}, f32[1]{0:T(128)}, u32[]{:S(2)}, u32[]{:S(2)}) collective-permute-start(f32[1]{0:T(128)} %add.20.refs_1_), channel_id=1, source_target_pairs={{0,4},{1,5},{2,6},{3,7},{4,0},{5,1},{6,2},{7,3},{8,12},{9,13},{10,... | collective-permute-start | bytes 20 | tf_op jit(solution)/shard_map/ppermute | solution.py:383
where the time goes:
time: 87.2 us; the launch traced here: 85.7 us
  waiting for transfers between devices  28.7 us (33%)
  Pallas kernels  27.5 us (32%)
  starting transfers between devices  20.8 us (24%)
  between operations  6.94 us (8%)
  local copies, waits for them, and re-layouts  1.05 us (1%)
    ppermute x4, waiting for transfers between devices, shifted(): return lax.ppermute(x, axis, [(i, (i + by) % peers) for i in range(peers)])  27.5 us
    pallas_call x2, Pallas kernels, grads(): pl.pallas_call(functools.partial(grad_kernel, pushed=not kept), out_shape...  17.5 us
    ppermute x4, starting transfers between devices, shifted(): return lax.ppermute(x, axis, [(i, (i + by) % peers) for i in range(peers)])  10.6 us
    ppermute x6, starting transfers between devices, other(): return lax.ppermute(x, axis, [(i, i ^ by) for i in range(peers)])  10.3 us
    pallas_call x1, Pallas kernels, local(): pl.pallas_call(functools.partial(push_kernel, room=room), out_shape=(plan...  4.15 us
    pallas_call x1, Pallas kernels, local(): pl.pallas_call(add_given_kernel, out_shape=shape(strip), in_specs=[smem,...  2.65 us
    pallas_call x1, Pallas kernels, local(): pl.pallas_call(add_returned_kernel, out_shape=shape(strip), in_specs=[sme...  1.92 us
  transfers between devices with their start and end apart: 10, of which 4 were waited for; matrix products, arithmetic and copies ran while one was open for 0% of the time, Pallas kernels for 23%

commit v1 on v0

--- a/solution.py
+++ b/solution.py
@@ -104,17 +104,18 @@
 
 def sizes(cap, width):
     whole = cap * width // UNIT
-    return whole * 5 // 16, whole // 4, whole * 5 // 16
-
-
-def make_plan(meta_ref, plan_ref, width, room):
+    first = (whole * 9 // 32, whole * 27 // 128, whole * 33 // 128)
+    return first, (whole * 5 // 16, whole // 4, whole * 5 // 16)
+
+
+def make_plan(meta_ref, plan_ref, width, rooms, again):
     cap = plan_ref.shape[1]
     units = width // UNIT
     seen_units = width // (UNIT * UNIT)
     shape = (UNIT, 128)
     choice = lax.broadcasted_iota(jnp.int32, shape, 0) * 128 + lax.broadcasted_iota(jnp.int32, shape, 1)
     zero = jnp.zeros(shape, jnp.int32)
-    push, back, pull, kept, bad = zero, zero, zero, zero, (choice >= (1 << cap)).astype(jnp.int32)
+    push, back, pull, n_push, bad = zero, zero, zero, zero, (choice >= (1 << cap)).astype(jnp.int32)
     count = meta_ref[0]
     for s in range(cap):
         row = meta_ref[1 + s]
@@ -124,11 +125,21 @@
         push += taken * (ahead + seen_units)
         back += taken * ahead
         pull += (1 - taken) * (crosses * ((row + UNIT - 1) // UNIT))
-        kept += 1 - taken
+        n_push += taken
         bad += taken * (1 - crosses)
-    bad += (push > room[0]).astype(jnp.int32) + (back > room[1]).astype(jnp.int32) + (pull > room[2]).astype(jnp.int32)
-    score = (kept + 16 * (bad > 0).astype(jnp.int32)) * (1 << cap) + choice
-    best = jnp.min(score.astype(jnp.float32)).astype(jnp.int32)
+    n_keep = count - n_push
+    groups = (n_push + BATCH - 1) // BATCH + (n_keep + BATCH - 1) // BATCH
+    worst = 16 * cap
+
+    def best_of(room):
+        over = bad + (push > room[0]).astype(jnp.int32) + (back > room[1]).astype(jnp.int32) + (pull > room[2]).astype(jnp.int32)
+        score = (groups * 16 + n_keep + worst * (over > 0).astype(jnp.int32)) * (1 << cap) + choice
+        return jnp.min(score.astype(jnp.float32)).astype(jnp.int32)
+
+    best = best_of(rooms[0])
+    short = (best >= worst << cap).astype(jnp.int32)
+    if again:
+        best = best_of(rooms[1])
     at_push = at_back = at_pull = n_pushed = n_kept = jnp.int32(0)
     for s in range(cap):
         plan_ref[PUSHED, s] = 0
@@ -136,8 +147,10 @@
         plan_ref[TOTALS, s] = 0
     for s in range(cap):
         row = meta_ref[1 + s]
-        taken = (best >> s) & 1
-        kept = jnp.where(s < count, 1 - taken, 0)
+        crosses = (row > 0).astype(jnp.int32)
+        now = short * crosses if again else 1 - short * crosses
+        taken = ((best >> s) & 1) * (short if again else 1 - short)
+        kept = jnp.where(s < count, (1 - taken) * now, 0)
         plan_ref[ROW, s] = row
         plan_ref[COL, s] = meta_ref[1 + cap + s]
         plan_ref[AT_PUSH, s] = at_push
@@ -160,6 +173,7 @@
         n_kept += kept
     plan_ref[TOTALS, 0] = n_pushed
     plan_ref[TOTALS, 1] = n_kept
+    plan_ref[TOTALS, 2] = short
 
 
 def pack(plan_ref, slot, own_ref, buffer_ref, start, first_unit, last_unit):
@@ -179,12 +193,17 @@
     lax.fori_loop(first_unit, last_unit, step, 0)
 
 
-def push_kernel(meta_ref, own_hbm, seen_hbm, plan_ref, push_ref, own_ref, sem, sems, *, room):
+def push_kernel(meta_ref, own_in_ref, seen_hbm, plan_ref, push_ref, *refs, rooms, again):
+    if again:
+        own_ref = own_in_ref
+        sems, = refs
+    else:
+        own_ref, left_ref, sem, sems = refs
+        load = pltpu.make_async_copy(own_in_ref, own_ref, sem)
+        load.start()
     width = own_ref.shape[2]
     units, seen_units = width // UNIT, seen_hbm.shape[1]
-    load = pltpu.make_async_copy(own_hbm, own_ref, sem)
-    load.start()
-    make_plan(meta_ref, plan_ref, width, room)
+    make_plan(meta_ref, plan_ref, width, rooms, again)
 
     def seen(i):
         slot = plan_ref[PUSHED, i]
@@ -211,10 +230,17 @@
     for r in range(plan_ref.shape[0]):
         for s in range(plan_ref.shape[1]):
             told = jnp.where(index == r * width + s, plan_ref[r, s].astype(jnp.float32), told)
-    push_ref[room[0], 0] = told
-    load.wait()
+    push_ref[push_ref.shape[0] - 1, 0] = told
+    if not again:
+        left_ref[...] = jnp.full(left_ref.shape, plan_ref[TOTALS, 2].astype(jnp.float32))
+        load.wait()
     lax.fori_loop(0, plan_ref[TOTALS, 0], step, 0)
     lax.fori_loop(0, plan_ref[TOTALS, 0], end, 0)
+
+
+def start_kernel(lefts_ref, grad_ref, left_ref):
+    grad_ref[...] = jnp.zeros_like(grad_ref)
+    left_ref[0] = jnp.sum(lefts_ref[...])
 
 
 def pull_kernel(told_ref, own_ref, plan_ref, pull_ref, whole_ref, numbers_ref, sem):
@@ -235,17 +261,16 @@
     lax.fori_loop(0, plan_ref[TOTALS, 1], step, 0)
 
 
-def grad_kernel(plan_ref, probe_ref, own_ref, came_ref, tables_ref, *refs, pushed):
+def grad_kernel(plan_ref, probe_ref, own_ref, came_ref, tables_ref, loss_in_ref, *refs, pushed):
     if pushed:
-        grad_ref, back_ref, loss_ref, wave_ref, window_ref = refs
+        grad_in_ref, grad_ref, back_ref, loss_ref, wave_ref, window_ref = refs
     else:
-        loss_in_ref, seen_ref, _, grad_ref, back_ref, loss_ref, wave_ref, window_ref = refs
+        grad_in_ref, seen_ref, grad_ref, back_ref, loss_ref, wave_ref, window_ref = refs
+    grad_ref[...] = grad_in_ref[...]
     slices, planes, width, columns = own_ref.shape
     units = width // UNIT
     seen_units = width // (UNIT * UNIT)
     last = came_ref.shape[0] - 1
-    if pushed:
-        grad_ref[...] = jnp.zeros_like(grad_ref)
     row_iota = lax.broadcasted_iota(jnp.int32, (width, width), 0)
     lane_iota = lax.broadcasted_iota(jnp.int32, (width, width), 1)
     count = plan_ref[TOTALS, 0 if pushed else 1]
@@ -304,12 +329,11 @@
 
         return loss
 
-    before = jnp.float32(0.0) if pushed else loss_in_ref[0]
-    loss_ref[0] = lax.fori_loop(0, (count + BATCH - 1) // BATCH, step, before)
-
-
-def after_kernel(x_ref, *refs):
-    pass
+    loss_ref[0] = lax.fori_loop(0, (count + BATCH - 1) // BATCH, step, loss_in_ref[0])
+
+
+def after_kernel(loss_ref, x_ref, first_ref, x_out_ref, losses_ref):
+    losses_ref[...] = jnp.full(losses_ref.shape, loss_ref[0])
 
 
 def add(plan, slot, grad_ref, layers, came, start, begin, end, below):
@@ -334,6 +358,7 @@
 
 def add_returned_kernel(plan_ref, returned_ref, grad_in_ref, grad_ref):
     slices, _, width, _ = grad_ref.shape
+    grad_ref[...] = grad_in_ref[...]
 
     def step(i, carry):
         slot = plan_ref[PUSHED, i]
@@ -344,19 +369,30 @@
     lax.fori_loop(0, plan_ref[TOTALS, 0], step, 0)
 
 
-def add_given_kernel(before_ref, given_ref, grad_ref, grad_hbm, sems):
+def add_given(before_ref, given_ref, grad_ref, layers):
+    def step(i, carry):
+        slot = before_ref[KEPT, i]
+        end = (before_ref[ROW, slot] + UNIT - 1) // UNIT
+        add(before_ref, slot, grad_ref, layers, given_ref, before_ref[AT_PULL, slot], 0, end, True)
+        return carry
+
+    lax.fori_loop(0, before_ref[TOTALS, 1], step, 0)
+
+
+def add_given_kernel(before_ref, given_ref, grad_in_ref, grad_ref):
+    grad_ref[...] = grad_in_ref[...]
+    add_given(before_ref, given_ref, grad_ref, range(grad_ref.shape[0]))
+
+
+def finish_kernel(before_ref, given_ref, losses_ref, grad_in_ref, grad_hbm, loss_ref, grad_ref, sems):
     slices = grad_ref.shape[0]
     stores = [pltpu.make_async_copy(grad_ref.at[l], grad_hbm.at[l], sems.at[l]) for l in range(slices)]
     for l in range(slices):
-
-        def step(i, carry, l=l):
-            slot = before_ref[KEPT, i]
-            end = (before_ref[ROW, slot] + UNIT - 1) // UNIT
-            add(before_ref, slot, grad_ref, [l], given_ref, before_ref[AT_PULL, slot], 0, end, True)
-            return carry
-
-        lax.fori_loop(0, before_ref[TOTALS, 1], step, 0)
+        grad_ref[l] = grad_in_ref[l]
+        add_given(before_ref, given_ref, grad_ref, [l])
         stores[l].start()
+    lanes = lax.broadcasted_iota(jnp.int32, losses_ref.shape, 1)
+    loss_ref[0] = jnp.sum(jnp.where(lanes == 0, losses_ref[...], 0.0))
     for store in stores:
         store.wait()
 
@@ -364,141 +400,117 @@
 def shifted(x, axis, by):
     peers = lax.axis_size(axis)
     return lax.ppermute(x, axis, [(i, (i + by) % peers) for i in range(peers)])
-
-
-def total_stages(peers):
-    stages, step = [], 1
-    while step < peers:
-        radix = 4 if step * 4 <= peers else 2
-        stages.append((step, radix))
-        step *= radix
-    return stages
-
-
-def partial_total(x, axis, stage):
-    peers = lax.axis_size(axis)
-    step, radix = stage
-
-    def other(by):
-        return lax.ppermute(x, axis, [(i, i ^ by) for i in range(peers)])
-
-    if radix == 2:
-        return x + other(step)
-    return (x + other(step)) + (other(2 * step) + other(3 * step))
 
 
 def local(probe_wave, object_slices, intensities, row_offset, col_offset, counts):
     width = probe_wave.shape[-1]
     slices, planes = object_slices.shape[:2]
     cap = row_offset.shape[0]
-    units = width // UNIT
-    seen_units = width // (UNIT * UNIT)
+    peers = lax.axis_size("tile")
+    units, seen_units = width // UNIT, width // (UNIT * UNIT)
     tables = jnp.asarray(make_tables(width))
+    meta = jnp.concatenate([counts, row_offset, col_offset])
     seen = intensities.reshape(cap, seen_units, UNIT, UNIT, width)
-    room = sizes(cap, width)
+    rooms = sizes(cap, width)
     smem = pl.BlockSpec(memory_space=pltpu.SMEM)
     vmem = pl.BlockSpec(memory_space=pltpu.VMEM)
-    hbm = pl.BlockSpec(memory_space=pltpu.HBM)
     anywhere = pl.BlockSpec(memory_space=pl.ANY)
     f32 = jnp.float32
 
-    def packed(n):
-        return (n, slices * planes, UNIT, width)
-
     def shape(dims, dtype=f32):
         return jax.ShapeDtypeStruct(dims, dtype)
 
-    def params(mib):
-        return pltpu.CompilerParams(vmem_limit_bytes=int(mib * 2**20))
-
-    def cost(us):
-        return pl.CostEstimate(flops=int(us * 1e9), bytes_accessed=int(us * 1e6), transcendentals=0)
-
-    strip = object_slices.shape
-    meta = jnp.concatenate([counts, row_offset, col_offset])
+    def packed(n):
+        return shape((n, slices * planes, UNIT, width))
+
+    def call(kernel, name, cost, ins, in_specs, outs, out_specs, scratch=(), mib=16, aliases=None):
+        return pl.pallas_call(
+            kernel,
+            out_shape=outs,
+            in_specs=in_specs,
+            out_specs=out_specs,
+            scratch_shapes=scratch,
+            input_output_aliases=aliases or {},
+            compiler_params=pltpu.CompilerParams(vmem_limit_bytes=mib << 20),
+            cost_estimate=pl.CostEstimate(flops=int(cost * 1e9), bytes_accessed=int(cost * 1e6), transcendentals=0),
+            name=name,
+        )(*ins)
+
+    strip = shape(object_slices.shape)
     plan_shape = shape((8, cap), jnp.int32)
-    plan, push, own = pl.pallas_call(
-        functools.partial(push_kernel, room=room),
-        out_shape=(plan_shape, shape(packed(room[0] + 1)), shape(strip)),
-        in_specs=[smem, hbm, hbm],
-        out_specs=(smem, vmem, vmem),
-        scratch_shapes=[pltpu.SemaphoreType.DMA, pltpu.SemaphoreType.DMA((cap,))],
-        compiler_params=params(48),
-        cost_estimate=cost(4),
-        name="pack_pushed",
-    )(meta, object_slices, seen)
+    rows = shape((peers, width))
+    one = shape((1,))
+    dma = pltpu.SemaphoreType.DMA
+
+    def ahead(source, again):
+        kernel = functools.partial(push_kernel, rooms=rooms, again=again)
+        ins, outs = (meta, source, seen), (plan_shape, packed(rooms[again][0] + 1))
+        if again:
+            return call(kernel, "pack_more", 4, ins, [smem, vmem, anywhere], outs, (smem, vmem), [dma((cap,))])
+        return call(
+            kernel, "pack_pushed", 4, ins, [smem, anywhere, anywhere], outs + (strip, rows), (smem, vmem, vmem, vmem),
+            [dma, dma((cap,))], 50,
+        )
+
+    def behind(pushed, own, again):
+        scratch = [pltpu.VMEM((UNIT, width), jnp.int32), pltpu.SMEM((UNIT, width), jnp.int32), dma]
+        outs = (plan_shape, packed(rooms[again][2]))
+        return call(pull_kernel, "pack_pulled", 2, (pushed, own), [vmem, vmem], outs, (smem, vmem), scratch)
+
+    def grads(plan, own, came, loss, grad, back, is_pushed):
+        name, more = ("grads_pushed", ()) if is_pushed else ("grads_kept", (intensities,))
+        buffer = pltpu.VMEM((BATCH, slices, planes, width, width), f32)
+        return call(
+            functools.partial(grad_kernel, pushed=is_pushed), name, 10,
+            (plan, probe_wave, own, came, tables, loss, grad) + more,
+            [smem] + [vmem] * 4 + [smem, vmem] + [vmem] * len(more),
+            (strip, packed(back), one), (vmem, vmem, smem), [buffer, buffer], 24, {6: 0},
+        )
+
+    def add_returned(plan, returned, grad):
+        return call(
+            add_returned_kernel, "add_returned", 1, (plan, returned, grad), [smem, vmem, vmem], strip, vmem, aliases={2: 0}
+        )
+
+    plan, push, own, left = ahead(object_slices, False)
     pushed = shifted(push, "tile", 1)
-    before, pull = pl.pallas_call(
-        pull_kernel,
-        out_shape=(plan_shape, shape(packed(room[2]))),
-        in_specs=[vmem, vmem],
-        out_specs=(smem, vmem),
-        scratch_shapes=[
-            pltpu.VMEM((UNIT, width), jnp.int32),
-            pltpu.SMEM((UNIT, width), jnp.int32),
-            pltpu.SemaphoreType.DMA,
-        ],
-        compiler_params=params(16),
-        cost_estimate=cost(2),
-        name="pack_pulled",
-    )(pushed, own)
+    lefts = lax.all_to_all(left, "tile", 0, 0, tiled=True)
+    before, pull = behind(pushed, own, False)
     pulled = shifted(pull, "tile", -1)
-
-    def grads(plan, came, back, *kept):
-        return pl.pallas_call(
-            functools.partial(grad_kernel, pushed=not kept),
-            out_shape=(shape(strip), shape(packed(back)), shape((1,))),
-            in_specs=[smem] + [vmem] * 4 + ([smem, vmem, vmem] if kept else []),
-            out_specs=(vmem, vmem, smem),
-            scratch_shapes=[
-                pltpu.VMEM((BATCH, slices, planes, width, width), f32),
-                pltpu.VMEM((BATCH, slices, planes, width, width), f32),
-            ],
-            input_output_aliases={7: 0} if kept else {},
-            compiler_params=params(24),
-            cost_estimate=cost(10),
-            name="grads_kept" if kept else "grads_pushed",
-        )(plan, probe_wave, own, came, tables, *kept)
-
-    grad, back, loss = grads(before, pushed, room[1])
+    grad, left = call(start_kernel, "start", 1, (lefts,), [vmem], (strip, one), (vmem, smem))
+
+    def unfinished(carry):
+        return carry[2][0] > 0
+
+    def second(carry):
+        grad, loss, _ = carry
+        plan, push = ahead(own, True)
+        pushed = shifted(push, "tile", 1)
+        before, pull = behind(pushed, own, True)
+        pulled = shifted(pull, "tile", -1)
+        grad, back, loss = grads(before, own, pushed, loss, grad, rooms[1][1], True)
+        returned = shifted(back, "tile", -1)
+        grad, back, loss = grads(plan, own, pulled, loss, grad, rooms[1][2], False)
+        given = shifted(back, "tile", 1)
+        grad = add_returned(plan, returned, grad)
+        grad = call(add_given_kernel, "add_given", 1, (before, given, grad), [smem, vmem, vmem], strip, vmem, aliases={2: 0})
+        return grad, loss, jnp.zeros_like(left)
+
+    grad, loss, _ = lax.while_loop(unfinished, second, (grad, jnp.zeros((1,), f32), left))
+    grad, back, loss = grads(before, own, pushed, loss, grad, rooms[0][1], True)
     returned = shifted(back, "tile", -1)
-    grad, back, loss = grads(plan, pulled, room[2], loss, intensities, grad)
-    stages = total_stages(lax.axis_size("tile"))
-    loss = partial_total(loss, "tile", stages[0])
-    back = pl.pallas_call(
-        after_kernel,
-        out_shape=shape(back.shape),
-        in_specs=[anywhere] * 3,
-        out_specs=anywhere,
-        input_output_aliases={0: 0},
-        compiler_params=params(4),
-        name="after_returned",
-    )(back, returned, loss)
+    grad, back, loss = grads(plan, own, pulled, loss, grad, rooms[0][2], False)
+    back, losses = call(
+        after_kernel, "after_returned", 1, (loss, back, returned), [smem, anywhere, anywhere],
+        (shape(back.shape), rows), (anywhere, vmem), aliases={1: 0},
+    )
     given = shifted(back, "tile", 1)
-    for stage in stages[1:]:
-        loss = partial_total(loss, "tile", stage)
-    misfit_total = loss.reshape(1)
-    grad = pl.pallas_call(
-        add_returned_kernel,
-        out_shape=shape(strip),
-        in_specs=[smem, vmem, vmem],
-        out_specs=vmem,
-        input_output_aliases={2: 0},
-        compiler_params=params(4),
-        cost_estimate=cost(1),
-        name="add_returned",
-    )(plan, returned, grad)
-    grad = pl.pallas_call(
-        add_given_kernel,
-        out_shape=shape(strip),
-        in_specs=[smem, vmem, vmem],
-        out_specs=hbm,
-        scratch_shapes=[pltpu.SemaphoreType.DMA((slices,))],
-        compiler_params=params(4),
-        cost_estimate=cost(4),
-        name="add_given",
-    )(before, given, grad)
-    return (grad, misfit_total)
+    losses = lax.all_to_all(losses, "tile", 0, 0, tiled=True)
+    grad = add_returned(plan, returned, grad)
+    return call(
+        finish_kernel, "add_given", 4, (before, given, losses, grad), [smem, vmem, vmem, vmem],
+        (strip, one), (anywhere, smem), [pltpu.VMEM(strip.shape, f32), dma((slices,))],
+    )
 
 
 def solution(mesh):

time: 87.2 us -> 82.3 us (0.944); the launches traced: 85.7 us -> 81.8 us
  Pallas kernels: 27.5 us -> 41.5 us
  waiting for transfers between devices: 28.7 us -> 21 us
  starting transfers between devices: 20.8 us -> 15.4 us
  between operations: 6.94 us -> 1.59 us
  loops' own time: 0 us -> 0.92 us
    ppermute x4, waiting for transfers between devices: 27.5 us -> 2.96 us  [shifted(): return lax.ppermute(x, axis, [(i, (i + by) % peers) for i in range(peers)])]
    all_to_all x0 -> x2, waiting for transfers between devices: none -> 18.1 us  [the longest x1 12.2 us: local(): lefts = lax.all_to_all(left, 'tile', 0, 0, tiled=True)]
    pallas_call x7 -> x8, Pallas kernels: 27.5 us -> 41.5 us  [call(): pl.pallas_call(kernel, out_shape=outs, in_specs=in_specs, out_specs=out_s...]
    all_to_all x0 -> x2, starting transfers between devices: none -> 12.9 us  [the longest x1 7.25 us: local(): lefts = lax.all_to_all(left, 'tile', 0, 0, tiled=True)]
    ppermute x6 -> x0, starting transfers between devices: 10.3 us -> none  [other(): return lax.ppermute(x, axis, [(i, i ^ by) for i in range(peers)])]
    ppermute x4, starting transfers between devices: 10.6 us -> 2.54 us  [shifted(): return lax.ppermute(x, axis, [(i, (i + by) % peers) for i in range(peers)])]
    ppermute x6 -> x0, waiting for transfers between devices: 1.13 us -> none  [other(): return lax.ppermute(x, axis, [(i, i ^ by) for i in range(peers)])]
    another operation x0 -> x1, loops' own time: none -> 0.92 us  [local(): lax.while_loop(unfinished, second, (grad, jnp.zeros((1,), f32), left))]
  transfers between devices with their start and end apart: 10 -> 6, of which waited for: 4 -> 3; matrix products, arithmetic and copies ran while one was open for 0% -> 0% of each run, Pallas kernels for 23% -> 31%
where the time goes in v1:
time: 82.3 us; the launch traced here: 81.8 us
  Pallas kernels  41.5 us (50%)
  waiting for transfers between devices  21 us (26%)
  starting transfers between devices  15.4 us (19%)
  between operations  1.59 us (2%)
  loops' own time  0.92 us (1%)
    pallas_call x8, Pallas kernels, call(): pl.pallas_call(kernel, out_shape=outs, in_specs=in_specs, out_specs=out_s...  41.5 us
    all_to_all x1, waiting for transfers between devices, local(): lefts = lax.all_to_all(left, 'tile', 0, 0, tiled=True)  12.2 us
    all_to_all x1, starting transfers between devices, local(): lefts = lax.all_to_all(left, 'tile', 0, 0, tiled=True)  7.25 us
    all_to_all x1, waiting for transfers between devices, local(): losses = lax.all_to_all(losses, 'tile', 0, 0, tiled=True)  5.89 us
    all_to_all x1, starting transfers between devices, local(): losses = lax.all_to_all(losses, 'tile', 0, 0, tiled=True)  5.61 us
    ppermute x4, waiting for transfers between devices, shifted(): return lax.ppermute(x, axis, [(i, (i + by) % peers) for i in range(peers)])  2.96 us
    ppermute x4, starting transfers between devices, shifted(): return lax.ppermute(x, axis, [(i, (i + by) % peers) for i in range(peers)])  2.54 us
  transfers between devices with their start and end apart: 6, of which 3 were waited for; matrix products, arithmetic and copies ran while one was open for 0% of the time, Pallas kernels for 31%

profile of v1, /device:TPU:0, one launch (start us, length us, event | category | flops | bytes accessed | tf_op | source)
XLA Modules:
  0.0 81.8 jit_solution(3608976036568129035)
XLA Ops:
  1.3 0.7 pad_add_fusion.meta_ref
  2.0 5.4 %pack_pushed.1 = (s32[8,8]{1,0:T(8,128)S(1)}, f32[37,8,8,128]{3,2,1,0:T(8,128)S(1)}, f32[4,2,128,1024]{3,2,1,0:T(8,128)}, f32[16,128]{1,0:T(8,128)}) custom-call(s32[17]{0:T(128)S(1)} %pad_add_fusion.meta_ref, f32[4,2,128,1024]{3,2,1,0:T(8,128)} %own_in_ref.1, f32[8,2,8,8,128]{4,3,2,1,0:T(8,128)} %bitcast.12), custom_call_target="tpu_custom_call" | custom-call | flops 4000000000 | bytes 4000000 | tf_op jit(solution)/shard_map/pack_pushed/pallas_call | solution.py:427
  7.4 0.4 collective-permute-start.4
  7.8 7.3 %all-to-all-start = ((f32[16,1,128]{2,1,0:T(1,128)}), f32[16,1,128]{2,1,0:T(1,128)S(1)}, u32[]{:S(2)}, u32[]{:S(2)}) async-start(f32[16,1,128]{2,1,0:T(1,128)} %bitcast.2), calls=%async_computation | async-start | bytes 16384 | tf_op jit(solution)/shard_map/all_to_all | solution.py:477
  15.0 12.2 %all-to-all-done = f32[16,1,128]{2,1,0:T(1,128)S(1)} async-done(((f32[16,1,128]{2,1,0:T(1,128)}), f32[16,1,128]{2,1,0:T(1,128)S(1)}, u32[]{:S(2)}, u32[]{:S(2)}) %all-to-all-start) | async-done | bytes 8224 | tf_op jit(solution)/shard_map/all_to_all | solution.py:477
  27.2 0.8 %start.1 = (f32[4,2,128,1024]{3,2,1,0:T(8,128)S(1)}, f32[1]{0:T(128)}) custom-call(f32[16,128]{1,0:T(8,128)S(1)} %bitcast.11), custom_call_target="tpu_custom_call" | custom-call | flops 1000000000 | bytes 1000000 | tf_op jit(solution)/shard_map/start/pallas_call | solution.py:427
  28.1 0.0 copy-start.3
  28.1 0.0 copy-start.4
  28.1 0.0 copy-start.5
  28.1 0.0 collective-permute-done.4.told_ref.came_ref
  28.1 4.0 %pack_pulled.2 = (s32[8,8]{1,0:T(8,128)S(1)}, f32[33,8,8,128]{3,2,1,0:T(8,128)}) custom-call(f32[37,8,8,128]{3,2,1,0:T(8,128)S(1)} %collective-permute-done.4.told_ref.came_ref, f32[4,2,128,1024]{3,2,1,0:T(8,128)} %get-tuple-element.166.own_ref), custom_call_target="tpu_custom_call" | custom-call | flops 2000000000 | bytes 2000000 | tf_op jit(solution)/shard_map/pack_pulled/pallas_call | solution.py:427
  32.1 2.1 %collective-permute-start.5 = (f32[33,8,8,128]{3,2,1,0:T(8,128)}, f32[33,8,8,128]{3,2,1,0:T(8,128)}, u32[]{:S(2)}, u32[]{:S(2)}) collective-permute-start(f32[33,8,8,128]{3,2,1,0:T(8,128)} %get-tuple-element.79), channel_id=1, source_target_pairs={{0,15},{1,0},{2,1},{3,2},{4,3},{5,4},{6,5},{7,6},{8,7},{9,8},{10,9... | collective-permute-start | bytes 3244040 | tf_op jit(solution)/shard_map/ppermute | solution.py:402
  34.2 0.0 copy-done.3
  34.2 0.0 copy-done.4
  34.2 0.0 copy-done.5
  34.2 0.0 copy-start
  34.2 0.9 %while.12 = (f32[4,2,128,1024]{3,2,1,0:T(8,128)S(1)}, f32[1]{0:T(128)}, f32[1]{0:T(128)}, s32[17]{0:T(128)S(1)}, f32[4,2,128,1024]{3,2,1,0:T(8,128)S(1)}, /*inde...) while((f32[4,2,128,1024]{3,2,1,0:T(8,128)S(1)}, f32[1]{0:T(128)}, ...), condition=%region_1.0_spmd.clone, body=%region_0.0_spmd.sunk.clone | while | flops 27999997952 | bytes 52248588 | solution.py:499
  35.1 0.3 copy-done
  35.4 8.7 %grads_pushed.2 = (f32[4,2,128,1024]{3,2,1,0:T(8,128)S(1)}, f32[27,8,8,128]{3,2,1,0:T(8,128)S(1)}, f32[1]{0:T(128)}) custom-call(s32[8,8]{1,0:T(8,128)S(1)} %get-tuple-element.77.plan_ref.before_ref, f32[2,128,128]{2,1,0:T(8,128)S(1)} %get-tuple-element.203, f32[4,2,128,1024]{3,2,1,0:T(8,128)S(1)} %get-tuple-element.204, ...), custom_call_target="tpu_custom_call", output_to_operand_aliasing={{0}: (6, {})} | custom-call | flops 10000000000 | bytes 10000000 | tf_op jit(solution)/shard_map/grads_pushed/pallas_call | solution.py:427
  44.2 0.1 collective-permute-start.6
  44.2 3.0 %collective-permute-done.5.came_ref = f32[33,8,8,128]{3,2,1,0:T(8,128)} collective-permute-done((f32[33,8,8,128]{3,2,1,0:T(8,128)}, f32[33,8,8,128]{3,2,1,0:T(8,128)}, u32[]{:S(2)}, u32[]{:S(2)}) %collective-permute-start.5) | collective-permute-done | bytes 1081376 | tf_op jit(solution)/shard_map/ppermute | solution.py:402
  47.2 10.4 %grads_kept.2 = (f32[4,2,128,1024]{3,2,1,0:T(8,128)S(1)}, f32[33,8,8,128]{3,2,1,0:T(8,128)S(1)}, f32[1]{0:T(128)}) custom-call(s32[8,8]{1,0:T(8,128)S(1)} %get-tuple-element.78.plan_ref, f32[2,128,128]{2,1,0:T(8,128)S(1)} %get-tuple-element.203, f32[4,2,128,1024]{3,2,1,0:T(8,128)S(1)} %get-tuple-element.204, ...), custom_call_target="tpu_custom_call", output_to_operand_aliasing={{0}: (6, {})} | custom-call | flops 10000000000 | bytes 10000000 | tf_op jit(solution)/shard_map/grads_kept/pallas_call | solution.py:427
  57.6 0.0 copy-start.2
  57.6 0.0 collective-permute-done.6.first_ref.returned_ref
  57.6 1.7 %after_returned.1 = (f32[33,8,8,128]{3,2,1,0:T(8,128)S(1)}, f32[16,128]{1,0:T(8,128)}) custom-call(f32[1]{0:T(128)} %get-tuple-element.87.loss_ref, f32[33,8,8,128]{3,2,1,0:T(8,128)S(1)} %get-tuple-element.88.x_ref, f32[27,8,8,128]{3,2,1,0:T(8,128)S(1)} %collective-permute-done.6.first_ref.returned_ref), custom_call_target="tpu_custom_call", output_to_operand_aliasing={{0}: (1, {})} | custom-call | flops 1000000000 | bytes 1000000 | tf_op jit(solution)/shard_map/after_returned/pallas_call | solution.py:427
  59.3 0.0 collective-permute-start.7
  59.3 0.2 copy-done.2
  59.5 5.6 %all-to-all-start.1 = ((f32[16,1,128]{2,1,0:T(1,128)}), f32[16,1,128]{2,1,0:T(1,128)S(1)}, u32[]{:S(2)}, u32[]{:S(2)}) async-start(f32[16,1,128]{2,1,0:T(1,128)} %bitcast.5), calls=%async_computation.1 | async-start | bytes 16384 | tf_op jit(solution)/shard_map/all_to_all | solution.py:508
  65.1 5.8 %add_returned.2.grad_in_ref = f32[4,2,128,1024]{3,2,1,0:T(8,128)} custom-call(s32[8,8]{1,0:T(8,128)S(1)} %get-tuple-element.78.plan_ref, f32[27,8,8,128]{3,2,1,0:T(8,128)S(1)} %collective-permute-done.6.first_ref.returned_ref, f32[4,2,128,1024]{3,2,1,0:T(8,128)} %copy-done.2), custom_call_target="tpu_custom_call", output_to_operand_aliasing={{}: (2, {})} | custom-call | flops 1000000000 | bytes 1000000 | tf_op jit(solution)/shard_map/add_returned/pallas_call | solution.py:427
  70.9 5.9 %all-to-all-done.1 = f32[16,1,128]{2,1,0:T(1,128)S(1)} async-done(((f32[16,1,128]{2,1,0:T(1,128)}), f32[16,1,128]{2,1,0:T(1,128)S(1)}, u32[]{:S(2)}, u32[]{:S(2)}) %all-to-all-start.1) | async-done | bytes 8224 | tf_op jit(solution)/shard_map/all_to_all | solution.py:508
  76.8 0.0 collective-permute-done.7.given_ref
  76.8 4.8 %add_given.2 = (f32[4,2,128,1024]{3,2,1,0:T(8,128)}, f32[1]{0:T(128)}) custom-call(s32[8,8]{1,0:T(8,128)S(1)} %get-tuple-element.77.plan_ref.before_ref, f32[33,8,8,128]{3,2,1,0:T(8,128)S(1)} %collective-permute-done.7.given_ref, f32[16,128]{1,0:T(8,128)S(1)} %bitcast.10, f32[4,2,128,1024]{3,2,1,0:T(8,128)} %add_returned.2.grad_in_ref), custom_call_target="tpu_custom_call" | custom-call | flops 4000000000 | bytes 4000000 | tf_op jit(solution)/shard_map/add_given/pallas_call | solution.py:427
Async XLA Ops:
  7.4 20.7 %collective-permute-start.4 = (f32[37,8,8,128]{3,2,1,0:T(8,128)S(1)}, f32[37,8,8,128]{3,2,1,0:T(8,128)S(1)}, u32[]{:S(2)}, u32[]{:S(2)}) collective-permute-start(f32[37,8,8,128]{3,2,1,0:T(8,128)S(1)} %get-tuple-element.75), channel_id=1, source_target_pairs={{0,1},{1,2},{2,3},{3,4},{4,5},{5,6},{6,7},{7,8},{8,9},{9,10},{10,1... | collective-permute-start | bytes 3637256 | tf_op jit(solution)/shard_map/ppermute | solution.py:402
  7.8 19.4 %all-to-all-start = ((f32[16,1,128]{2,1,0:T(1,128)}), f32[16,1,128]{2,1,0:T(1,128)S(1)}, u32[]{:S(2)}, u32[]{:S(2)}) async-start(f32[16,1,128]{2,1,0:T(1,128)} %bitcast.2), calls=%async_computation | async-start | bytes 16384 | tf_op jit(solution)/shard_map/all_to_all | solution.py:477
  28.1 6.1 %copy-start.3 = (f32[8,128,128]{2,1,0:T(8,128)S(1)}, f32[8,128,128]{2,1,0:T(8,128)}, u32[]{:S(2)}) copy-start(f32[8,128,128]{2,1,0:T(8,128)} %refs_1_.1) | copy-start | bytes 1572868
  28.1 6.1 %copy-start.4 = (f32[2,128,128]{2,1,0:T(8,128)S(1)}, f32[2,128,128]{2,1,0:T(8,128)}, u32[]{:S(2)}) copy-start(f32[2,128,128]{2,1,0:T(8,128)} %probe_ref.3) | copy-start | bytes 393220
  28.1 6.1 %copy-start.5 = (f32[4,2,128,1024]{3,2,1,0:T(8,128)S(1)}, f32[4,2,128,1024]{3,2,1,0:T(8,128)}, u32[]{:S(2)}) copy-start(f32[4,2,128,1024]{3,2,1,0:T(8,128)} %get-tuple-element.166.own_ref) | copy-start | bytes 12582916
  32.1 15.1 %collective-permute-start.5 = (f32[33,8,8,128]{3,2,1,0:T(8,128)}, f32[33,8,8,128]{3,2,1,0:T(8,128)}, u32[]{:S(2)}, u32[]{:S(2)}) collective-permute-start(f32[33,8,8,128]{3,2,1,0:T(8,128)} %get-tuple-element.79), channel_id=1, source_target_pairs={{0,15},{1,0},{2,1},{3,2},{4,3},{5,4},{6,5},{7,6},{8,7},{9,8},{10,9... | collective-permute-start | bytes 3244040 | tf_op jit(solution)/shard_map/ppermute | solution.py:402
  34.2 1.2 %copy-start = (bf16[2,2,2,256,256]{4,3,2,1,0:T(8,128)(2,1)S(1)}, bf16[2,2,2,256,256]{4,3,2,1,0:T(8,128)(2,1)}, u32[]{:S(2)}) copy-start(bf16[2,2,2,256,256]{4,3,2,1,0:T(8,128)(2,1)} %constant.9.clone.tables_ref) | copy-start | bytes 3145732
  44.2 13.4 %collective-permute-start.6 = (f32[27,8,8,128]{3,2,1,0:T(8,128)S(1)}, f32[27,8,8,128]{3,2,1,0:T(8,128)S(1)}, u32[]{:S(2)}, u32[]{:S(2)}) collective-permute-start(f32[27,8,8,128]{3,2,1,0:T(8,128)S(1)} %get-tuple-element.89), channel_id=1, source_target_pairs={{0,15},{1,0},{2,1},{3,2},{4,3},{5,4},{6,5},{7,6},{8,7},{9,8},{10,9... | collective-permute-start | bytes 2654216 | tf_op jit(solution)/shard_map/ppermute | solution.py:402
  57.6 1.9 %copy-start.2 = (f32[4,2,128,1024]{3,2,1,0:T(8,128)}, f32[4,2,128,1024]{3,2,1,0:T(8,128)S(1)}, u32[]{:S(2)}) copy-start(f32[4,2,128,1024]{3,2,1,0:T(8,128)S(1)} %get-tuple-element.92.grad_in_ref) | copy-start | bytes 12582916
  59.3 17.5 %collective-permute-start.7 = (f32[33,8,8,128]{3,2,1,0:T(8,128)S(1)}, f32[33,8,8,128]{3,2,1,0:T(8,128)S(1)}, u32[]{:S(2)}, u32[]{:S(2)}) collective-permute-start(f32[33,8,8,128]{3,2,1,0:T(8,128)S(1)} %get-tuple-element.90), channel_id=1, source_target_pairs={{0,1},{1,2},{2,3},{3,4},{4,5},{5,6},{6,7},{7,8},{8,9},{9,10},{10,1... | collective-permute-start | bytes 3244040 | tf_op jit(solution)/shard_map/ppermute | solution.py:402
  59.5 17.3 %all-to-all-start.1 = ((f32[16,1,128]{2,1,0:T(1,128)}), f32[16,1,128]{2,1,0:T(1,128)S(1)}, u32[]{:S(2)}, u32[]{:S(2)}) async-start(f32[16,1,128]{2,1,0:T(1,128)} %bitcast.5), calls=%async_computation.1 | async-start | bytes 16384 | tf_op jit(solution)/shard_map/all_to_all | solution.py:508

commit v2 on v1

--- a/solution.py
+++ b/solution.py
@@ -238,7 +238,7 @@
     lax.fori_loop(0, plan_ref[TOTALS, 0], end, 0)
 
 
-def start_kernel(lefts_ref, grad_ref, left_ref):
+def start_kernel(lefts_ref, plan_ref, grad_ref, left_ref):
     grad_ref[...] = jnp.zeros_like(grad_ref)
     left_ref[0] = jnp.sum(lefts_ref[...])
 
@@ -436,6 +436,9 @@
             name=name,
         )(*ins)
 
+    def held(like):
+        return pltpu.VMEM(like.shape, like.dtype)
+
     strip = shape(object_slices.shape)
     plan_shape = shape((8, cap), jnp.int32)
     rows = shape((peers, width))
@@ -444,17 +447,17 @@
 
     def ahead(source, again):
         kernel = functools.partial(push_kernel, rooms=rooms, again=again)
-        ins, outs = (meta, source, seen), (plan_shape, packed(rooms[again][0] + 1))
+        ins, outs = (meta, source, seen), (plan_shape, held(packed(rooms[again][0] + 1)))
         if again:
             return call(kernel, "pack_more", 4, ins, [smem, vmem, anywhere], outs, (smem, vmem), [dma((cap,))])
         return call(
-            kernel, "pack_pushed", 4, ins, [smem, anywhere, anywhere], outs + (strip, rows), (smem, vmem, vmem, vmem),
-            [dma, dma((cap,))], 50,
+            kernel, "pack_pushed", 4, (meta,) + tuple(pltpu.with_memory_space_constraint(x, pltpu.HBM) for x in (source, seen)),
+            [smem, anywhere, anywhere], outs + (held(strip), rows), (smem, vmem, vmem, vmem), [dma, dma((cap,))],
         )
 
     def behind(pushed, own, again):
         scratch = [pltpu.VMEM((UNIT, width), jnp.int32), pltpu.SMEM((UNIT, width), jnp.int32), dma]
-        outs = (plan_shape, packed(rooms[again][2]))
+        outs = (plan_shape, held(packed(rooms[again][2])))
         return call(pull_kernel, "pack_pulled", 2, (pushed, own), [vmem, vmem], outs, (smem, vmem), scratch)
 
     def grads(plan, own, came, loss, grad, back, is_pushed):
@@ -464,12 +467,12 @@
             functools.partial(grad_kernel, pushed=is_pushed), name, 10,
             (plan, probe_wave, own, came, tables, loss, grad) + more,
             [smem] + [vmem] * 4 + [smem, vmem] + [vmem] * len(more),
-            (strip, packed(back), one), (vmem, vmem, smem), [buffer, buffer], 24, {6: 0},
+            (held(strip), held(packed(back)), one), (vmem, vmem, smem), [buffer, buffer], 24, {6: 0},
         )
 
     def add_returned(plan, returned, grad):
         return call(
-            add_returned_kernel, "add_returned", 1, (plan, returned, grad), [smem, vmem, vmem], strip, vmem, aliases={2: 0}
+            add_returned_kernel, "add_returned", 1, (plan, returned, grad), [smem, vmem, vmem], held(strip), vmem, aliases={2: 0}
         )
 
     plan, push, own, left = ahead(object_slices, False)
@@ -477,7 +480,7 @@
     lefts = lax.all_to_all(left, "tile", 0, 0, tiled=True)
     before, pull = behind(pushed, own, False)
     pulled = shifted(pull, "tile", -1)
-    grad, left = call(start_kernel, "start", 1, (lefts,), [vmem], (strip, one), (vmem, smem))
+    grad, left = call(start_kernel, "start", 1, (lefts, before), [vmem, smem], (held(strip), one), (vmem, smem))
 
     def unfinished(carry):
         return carry[2][0] > 0
@@ -493,7 +496,7 @@
         grad, back, loss = grads(plan, own, pulled, loss, grad, rooms[1][2], False)
         given = shifted(back, "tile", 1)
         grad = add_returned(plan, returned, grad)
-        grad = call(add_given_kernel, "add_given", 1, (before, given, grad), [smem, vmem, vmem], strip, vmem, aliases={2: 0})
+        grad = call(add_given_kernel, "add_given", 1, (before, given, grad), [smem, vmem, vmem], held(strip), vmem, aliases={2: 0})
         return grad, loss, jnp.zeros_like(left)
 
     grad, loss, _ = lax.while_loop(unfinished, second, (grad, jnp.zeros((1,), f32), left))
@@ -502,7 +505,7 @@
     grad, back, loss = grads(plan, own, pulled, loss, grad, rooms[0][2], False)
     back, losses = call(
         after_kernel, "after_returned", 1, (loss, back, returned), [smem, anywhere, anywhere],
-        (shape(back.shape), rows), (anywhere, vmem), aliases={1: 0},
+        (held(back), rows), (anywhere, vmem), aliases={1: 0},
     )
     given = shifted(back, "tile", 1)
     losses = lax.all_to_all(losses, "tile", 0, 0, tiled=True)

time: 82.3 us -> 82.6 us (level)
  Pallas kernels: 41.5 us -> 32.2 us
  local copies, waits for them, and re-layouts: 0.53 us -> 8.46 us
  waiting for transfers between devices: 21 us -> 22.9 us
    ppermute x4, waiting for transfers between devices: 2.96 us -> 17.9 us  [shifted(): return lax.ppermute(x, axis, [(i, (i + by) % peers) for i in range(peers)])]
    all_to_all x1, waiting for transfers between devices: 12.2 us -> 0.01 us  [local(): lefts = lax.all_to_all(left, 'tile', 0, 0, tiled=True)]
    pallas_call x8, Pallas kernels: 41.5 us -> 32.2 us  [call(): pl.pallas_call(kernel, out_shape=outs, in_specs=in_specs, out_specs=out_s...]
    unnamed x10 -> x20, local copies, waits for them, and re-layouts: 0.53 us -> 8.46 us
    all_to_all x1, waiting for transfers between devices: 5.89 us -> 4.98 us  [local(): losses = lax.all_to_all(losses, 'tile', 0, 0, tiled=True)]
  transfers between devices with their start and end apart: 6 -> 6, of which waited for: 3 -> 3; matrix products, arithmetic and copies ran while one was open for 0% -> 0% of each run, Pallas kernels for 31% -> 26%
where the time goes in v2:
time: 82.6 us; the launch traced here: 81.9 us
  Pallas kernels  32.2 us (39%)
  waiting for transfers between devices  22.9 us (28%)
  starting transfers between devices  15 us (18%)
  local copies, waits for them, and re-layouts  8.46 us (10%)
  between operations  1.65 us (2%)
  loops' own time  0.92 us (1%)
    pallas_call x8, Pallas kernels, call(): pl.pallas_call(kernel, out_shape=outs, in_specs=in_specs, out_specs=out_s...  32.2 us
    ppermute x4, waiting for transfers between devices, shifted(): return lax.ppermute(x, axis, [(i, (i + by) % peers) for i in range(peers)])  17.9 us
    unnamed x20, local copies, waits for them, and re-layouts  8.46 us
    all_to_all x1, starting transfers between devices, local(): lefts = lax.all_to_all(left, 'tile', 0, 0, tiled=True)  6.85 us
    all_to_all x1, starting transfers between devices, local(): losses = lax.all_to_all(losses, 'tile', 0, 0, tiled=True)  5.24 us
    all_to_all x1, waiting for transfers between devices, local(): losses = lax.all_to_all(losses, 'tile', 0, 0, tiled=True)  4.98 us
    ppermute x4, starting transfers between devices, shifted(): return lax.ppermute(x, axis, [(i, (i + by) % peers) for i in range(peers)])  2.86 us
  transfers between devices with their start and end apart: 6, of which 3 were waited for; matrix products, arithmetic and copies ran while one was open for 0% of the time, Pallas kernels for 26%

profile of v2, /device:TPU:0, one launch (start us, length us, event | category | flops | bytes accessed | tf_op | source)
XLA Modules:
  0.0 81.9 jit_solution(17749433171161701320)
XLA Ops:
  1.3 0.7 pad_add_fusion.meta_ref
  2.0 4.0 %pack_pushed.1 = (s32[8,8]{1,0:T(8,128)S(1)}, f32[37,8,8,128]{3,2,1,0:T(8,128)S(1)}, f32[4,2,128,1024]{3,2,1,0:T(8,128)S(1)}, f32[16,128]{1,0:T(8,128)}) custom-call(s32[17]{0:T(128)S(1)} %pad_add_fusion.meta_ref, f32[4,2,128,1024]{3,2,1,0:T(8,128)} %own_in_ref.1, f32[8,2,8,8,128]{4,3,2,1,0:T(8,128)} %bitcast.12), custom_call_target="tpu_custom_call" | custom-call | flops 4000000000 | bytes 4000000 | tf_op jit(solution)/shard_map/pack_pushed/pallas_call | solution.py:427
  6.0 0.0 copy-start.3
  6.1 2.0 %copy-done.3 = f32[4,2,128,1024]{3,2,1,0:T(8,128)} copy-done((f32[4,2,128,1024]{3,2,1,0:T(8,128)}, f32[4,2,128,1024]{3,2,1,0:T(8,128)S(1)}, u32[]{:S(2)}) %copy-start.3) | copy-done | bytes 4194328
  8.1 0.4 collective-permute-start.4
  8.4 6.9 %all-to-all-start = ((f32[16,1,128]{2,1,0:T(1,128)}), f32[16,1,128]{2,1,0:T(1,128)S(1)}, u32[]{:S(2)}, u32[]{:S(2)}) async-start(f32[16,1,128]{2,1,0:T(1,128)} %bitcast.2), calls=%async_computation | async-start | bytes 16384 | tf_op jit(solution)/shard_map/all_to_all | solution.py:480
  15.3 12.6 %collective-permute-done.4.told_ref.came_ref = f32[37,8,8,128]{3,2,1,0:T(8,128)S(1)} collective-permute-done((f32[37,8,8,128]{3,2,1,0:T(8,128)S(1)}, f32[37,8,8,128]{3,2,1,0:T(8,128)S(1)}, u32[]{:S(2)}, u32[]{:S(2)}) %collective-permute-start.4) | collective-permute-done | bytes 1212448 | tf_op jit(solution)/shard_map/ppermute | solution.py:402
  27.9 4.3 %pack_pulled.2 = (s32[8,8]{1,0:T(8,128)S(1)}, f32[33,8,8,128]{3,2,1,0:T(8,128)}) custom-call(f32[37,8,8,128]{3,2,1,0:T(8,128)S(1)} %collective-permute-done.4.told_ref.came_ref, f32[4,2,128,1024]{3,2,1,0:T(8,128)} %copy-done.3), custom_call_target="tpu_custom_call" | custom-call | flops 2000000000 | bytes 2000000 | tf_op jit(solution)/shard_map/pack_pulled/pallas_call | solution.py:427
  32.1 0.0 copy-start.8
  32.1 0.1 collective-permute-start.5
  32.2 0.0 all-to-all-done
  32.2 1.4 %start.1 = (f32[4,2,128,1024]{3,2,1,0:T(8,128)S(1)}, f32[1]{0:T(128)}) custom-call(f32[16,128]{1,0:T(8,128)S(1)} %bitcast.10, s32[8,8]{1,0:T(8,128)S(1)} %get-tuple-element.77.plan_ref.before_ref), custom_call_target="tpu_custom_call" | custom-call | flops 1000000000 | bytes 1000000 | tf_op jit(solution)/shard_map/start/pallas_call | solution.py:427
  33.7 0.0 copy-start.6
  33.7 0.9 %while.12 = (f32[4,2,128,1024]{3,2,1,0:T(8,128)S(1)}, f32[1]{0:T(128)}, f32[1]{0:T(128)}, s32[17]{0:T(128)S(1)}, f32[4,2,128,1024]{3,2,1,0:T(8,128)}, /*index=5*...) while((f32[4,2,128,1024]{3,2,1,0:T(8,128)S(1)}, f32[1]{0:T(128)}, ...), condition=%region_1.0_spmd.clone, body=%region_0.0_spmd.sunk.clone | while | flops 27999997952 | bytes 69025832 | solution.py:502
  34.6 0.3 copy-done.6
  34.9 10.6 %grads_pushed.2 = (f32[4,2,128,1024]{3,2,1,0:T(8,128)S(1)}, f32[27,8,8,128]{3,2,1,0:T(8,128)S(1)}, f32[1]{0:T(128)}) custom-call(s32[8,8]{1,0:T(8,128)S(1)} %get-tuple-element.77.plan_ref.before_ref, f32[2,128,128]{2,1,0:T(8,128)S(1)} %get-tuple-element.204, f32[4,2,128,1024]{3,2,1,0:T(8,128)} %get-tuple-element.202, ...), custom_call_target="tpu_custom_call", output_to_operand_aliasing={{0}: (6, {})} | custom-call | flops 10000000000 | bytes 10000000 | tf_op jit(solution)/shard_map/grads_pushed/pallas_call | solution.py:427
  45.5 0.1 collective-permute-start.6
  45.6 0.0 collective-permute-done.5.came_ref
  45.6 3.2 %grads_kept.2 = (f32[4,2,128,1024]{3,2,1,0:T(8,128)S(1)}, f32[33,8,8,128]{3,2,1,0:T(8,128)S(1)}, f32[1]{0:T(128)}) custom-call(s32[8,8]{1,0:T(8,128)S(1)} %get-tuple-element.78.plan_ref, f32[2,128,128]{2,1,0:T(8,128)S(1)} %get-tuple-element.204, f32[4,2,128,1024]{3,2,1,0:T(8,128)S(1)} %copy-done.5, ...), custom_call_target="tpu_custom_call", output_to_operand_aliasing={{0}: (6, {})} | custom-call | flops 10000000000 | bytes 10000000 | tf_op jit(solution)/shard_map/grads_kept/pallas_call | solution.py:427
  48.8 0.0 copy-start
  48.8 2.0 %copy-done = f32[4,2,128,1024]{3,2,1,0:T(8,128)} copy-done((f32[4,2,128,1024]{3,2,1,0:T(8,128)}, f32[4,2,128,1024]{3,2,1,0:T(8,128)S(1)}, u32[]{:S(2)}) %copy-start) | copy-done | bytes 4194328
  50.8 5.3 %collective-permute-done.6.first_ref.returned_ref = f32[27,8,8,128]{3,2,1,0:T(8,128)S(1)} collective-permute-done((f32[27,8,8,128]{3,2,1,0:T(8,128)S(1)}, f32[27,8,8,128]{3,2,1,0:T(8,128)S(1)}, u32[]{:S(2)}, u32[]{:S(2)}) %collective-permute-start.6) | collective-permute-done | bytes 884768 | tf_op jit(solution)/shard_map/ppermute | solution.py:402
  56.2 1.2 %after_returned.1 = (f32[33,8,8,128]{3,2,1,0:T(8,128)S(1)}, f32[16,128]{1,0:T(8,128)}) custom-call(f32[1]{0:T(128)} %get-tuple-element.87.loss_ref, f32[33,8,8,128]{3,2,1,0:T(8,128)S(1)} %get-tuple-element.88.x_ref, f32[27,8,8,128]{3,2,1,0:T(8,128)S(1)} %collective-permute-done.6.first_ref.returned_ref), custom_call_target="tpu_custom_call", output_to_operand_aliasing={{0}: (1, {})} | custom-call | flops 1000000000 | bytes 1000000 | tf_op jit(solution)/shard_map/after_returned/pallas_call | solution.py:427
  57.4 2.4 %collective-permute-start.7 = (f32[33,8,8,128]{3,2,1,0:T(8,128)S(1)}, f32[33,8,8,128]{3,2,1,0:T(8,128)S(1)}, u32[]{:S(2)}, u32[]{:S(2)}) collective-permute-start(f32[33,8,8,128]{3,2,1,0:T(8,128)S(1)} %get-tuple-element.90), channel_id=1, source_target_pairs={{0,1},{1,2},{2,3},{3,4},{4,5},{5,6},{6,7},{7,8},{8,9},{9,10},{10,1... | collective-permute-start | bytes 3244040 | tf_op jit(solution)/shard_map/ppermute | solution.py:402
  59.7 5.2 %all-to-all-start.1 = ((f32[16,1,128]{2,1,0:T(1,128)}), f32[16,1,128]{2,1,0:T(1,128)S(1)}, u32[]{:S(2)}, u32[]{:S(2)}) async-start(f32[16,1,128]{2,1,0:T(1,128)} %bitcast.5), calls=%async_computation.1 | async-start | bytes 16384 | tf_op jit(solution)/shard_map/all_to_all | solution.py:511
  65.0 0.0 copy-start.1
  65.0 2.2 %copy-done.1 = f32[4,2,128,1024]{3,2,1,0:T(8,128)S(1)} copy-done((f32[4,2,128,1024]{3,2,1,0:T(8,128)S(1)}, f32[4,2,128,1024]{3,2,1,0:T(8,128)}, u32[]{:S(2)}) %copy-start.1) | copy-done | bytes 4194328
  67.2 2.1 %add_returned.2.grad_in_ref = f32[4,2,128,1024]{3,2,1,0:T(8,128)S(1)} custom-call(s32[8,8]{1,0:T(8,128)S(1)} %get-tuple-element.78.plan_ref, f32[27,8,8,128]{3,2,1,0:T(8,128)S(1)} %collective-permute-done.6.first_ref.returned_ref, f32[4,2,128,1024]{3,2,1,0:T(8,128)S(1)} %copy-done.1), custom_call_target="tpu_custom_call", output_to_operand_aliasing={{}: (2, {})} | custom-call | flops 1000000000 | bytes 1000000 | tf_op jit(solution)/shard_map/add_returned/pallas_call | solution.py:427
  69.3 1.9 %copy-done.2 = f32[4,2,128,1024]{3,2,1,0:T(8,128)} copy-done((f32[4,2,128,1024]{3,2,1,0:T(8,128)}, f32[4,2,128,1024]{3,2,1,0:T(8,128)S(1)}, u32[]{:S(2)}) %copy-start.2) | copy-done | bytes 4194328
  71.3 5.0 %all-to-all-done.1 = f32[16,1,128]{2,1,0:T(1,128)S(1)} async-done(((f32[16,1,128]{2,1,0:T(1,128)}), f32[16,1,128]{2,1,0:T(1,128)S(1)}, u32[]{:S(2)}, u32[]{:S(2)}) %all-to-all-start.1) | async-done | bytes 8224 | tf_op jit(solution)/shard_map/all_to_all | solution.py:511
  76.3 0.0 collective-permute-done.7.given_ref
  76.3 5.4 %add_given.2 = (f32[4,2,128,1024]{3,2,1,0:T(8,128)}, f32[1]{0:T(128)}) custom-call(s32[8,8]{1,0:T(8,128)S(1)} %copy-done.9, f32[33,8,8,128]{3,2,1,0:T(8,128)S(1)} %collective-permute-done.7.given_ref, f32[16,128]{1,0:T(8,128)S(1)} %bitcast.11, f32[4,2,128,1024]{3,2,1,0:T(8,128)} %copy-done.2), custom_call_target="tpu_custom_call" | custom-call | flops 4000000000 | bytes 4000000 | tf_op jit(solution)/shard_map/add_given/pallas_call | solution.py:427
  (10 shorter events, 0.0 us)
Async XLA Ops:
  6.0 2.0 %copy-start.3 = (f32[4,2,128,1024]{3,2,1,0:T(8,128)}, f32[4,2,128,1024]{3,2,1,0:T(8,128)S(1)}, u32[]{:S(2)}) copy-start(f32[4,2,128,1024]{3,2,1,0:T(8,128)S(1)} %get-tuple-element.166.own_ref) | copy-start | bytes 12582916
  8.1 19.8 %collective-permute-start.4 = (f32[37,8,8,128]{3,2,1,0:T(8,128)S(1)}, f32[37,8,8,128]{3,2,1,0:T(8,128)S(1)}, u32[]{:S(2)}, u32[]{:S(2)}) collective-permute-start(f32[37,8,8,128]{3,2,1,0:T(8,128)S(1)} %get-tuple-element.75), channel_id=1, source_target_pairs={{0,1},{1,2},{2,3},{3,4},{4,5},{5,6},{6,7},{7,8},{8,9},{9,10},{10,1... | collective-permute-start | bytes 3637256 | tf_op jit(solution)/shard_map/ppermute | solution.py:402
  8.4 23.8 %all-to-all-start = ((f32[16,1,128]{2,1,0:T(1,128)}), f32[16,1,128]{2,1,0:T(1,128)S(1)}, u32[]{:S(2)}, u32[]{:S(2)}) async-start(f32[16,1,128]{2,1,0:T(1,128)} %bitcast.2), calls=%async_computation | async-start | bytes 16384 | tf_op jit(solution)/shard_map/all_to_all | solution.py:480
  27.9 5.8 %copy-start.10 = (f32[8,128,128]{2,1,0:T(8,128)S(1)}, f32[8,128,128]{2,1,0:T(8,128)}, u32[]{:S(2)}) copy-start(f32[8,128,128]{2,1,0:T(8,128)} %refs_1_.1) | copy-start | bytes 1572868
  27.9 5.8 %copy-start.11 = (f32[2,128,128]{2,1,0:T(8,128)S(1)}, f32[2,128,128]{2,1,0:T(8,128)}, u32[]{:S(2)}) copy-start(f32[2,128,128]{2,1,0:T(8,128)} %probe_ref.3) | copy-start | bytes 393220
  32.1 2.5 %copy-start.8 = (s32[8,8]{1,0:T(8,128)}, s32[8,8]{1,0:T(8,128)S(1)}, u32[]{:S(2)}) copy-start(s32[8,8]{1,0:T(8,128)S(1)} %get-tuple-element.77.plan_ref.before_ref) | copy-start | bytes 772
  32.1 13.5 %collective-permute-start.5 = (f32[33,8,8,128]{3,2,1,0:T(8,128)}, f32[33,8,8,128]{3,2,1,0:T(8,128)}, u32[]{:S(2)}, u32[]{:S(2)}) collective-permute-start(f32[33,8,8,128]{3,2,1,0:T(8,128)} %get-tuple-element.79), channel_id=1, source_target_pairs={{0,15},{1,0},{2,1},{3,2},{4,3},{5,4},{6,5},{7,6},{8,7},{9,8},{10,9... | collective-permute-start | bytes 3244040 | tf_op jit(solution)/shard_map/ppermute | solution.py:402
  33.7 1.2 %copy-start.6 = (bf16[2,2,2,256,256]{4,3,2,1,0:T(8,128)(2,1)S(1)}, bf16[2,2,2,256,256]{4,3,2,1,0:T(8,128)(2,1)}, u32[]{:S(2)}) copy-start(bf16[2,2,2,256,256]{4,3,2,1,0:T(8,128)(2,1)} %constant.9.clone.tables_ref) | copy-start | bytes 3145732
  34.9 10.7 %copy-start.5 = (f32[4,2,128,1024]{3,2,1,0:T(8,128)S(1)}, f32[4,2,128,1024]{3,2,1,0:T(8,128)}, u32[]{:S(2)}) copy-start(f32[4,2,128,1024]{3,2,1,0:T(8,128)} %get-tuple-element.202) | copy-start | bytes 12582916
  45.5 10.6 %collective-permute-start.6 = (f32[27,8,8,128]{3,2,1,0:T(8,128)S(1)}, f32[27,8,8,128]{3,2,1,0:T(8,128)S(1)}, u32[]{:S(2)}, u32[]{:S(2)}) collective-permute-start(f32[27,8,8,128]{3,2,1,0:T(8,128)S(1)} %get-tuple-element.89), channel_id=1, source_target_pairs={{0,15},{1,0},{2,1},{3,2},{4,3},{5,4},{6,5},{7,6},{8,7},{9,8},{10,9... | collective-permute-start | bytes 2654216 | tf_op jit(solution)/shard_map/ppermute | solution.py:402
  48.8 2.0 %copy-start = (f32[4,2,128,1024]{3,2,1,0:T(8,128)}, f32[4,2,128,1024]{3,2,1,0:T(8,128)S(1)}, u32[]{:S(2)}) copy-start(f32[4,2,128,1024]{3,2,1,0:T(8,128)S(1)} %get-tuple-element.92.grad_in_ref) | copy-start | bytes 12582916
  57.4 18.9 %collective-permute-start.7 = (f32[33,8,8,128]{3,2,1,0:T(8,128)S(1)}, f32[33,8,8,128]{3,2,1,0:T(8,128)S(1)}, u32[]{:S(2)}, u32[]{:S(2)}) collective-permute-start(f32[33,8,8,128]{3,2,1,0:T(8,128)S(1)} %get-tuple-element.90), channel_id=1, source_target_pairs={{0,1},{1,2},{2,3},{3,4},{4,5},{5,6},{6,7},{7,8},{8,9},{9,10},{10,1... | collective-permute-start | bytes 3244040 | tf_op jit(solution)/shard_map/ppermute | solution.py:402
  59.7 16.5 %all-to-all-start.1 = ((f32[16,1,128]{2,1,0:T(1,128)}), f32[16,1,128]{2,1,0:T(1,128)S(1)}, u32[]{:S(2)}, u32[]{:S(2)}) async-start(f32[16,1,128]{2,1,0:T(1,128)} %bitcast.5), calls=%async_computation.1 | async-start | bytes 16384 | tf_op jit(solution)/shard_map/all_to_all | solution.py:511
  65.0 2.2 %copy-start.1 = (f32[4,2,128,1024]{3,2,1,0:T(8,128)S(1)}, f32[4,2,128,1024]{3,2,1,0:T(8,128)}, u32[]{:S(2)}) copy-start(f32[4,2,128,1024]{3,2,1,0:T(8,128)} %copy-done) | copy-start | bytes 12582916
  67.2 9.1 %copy-start.9 = (s32[8,8]{1,0:T(8,128)S(1)}, s32[8,8]{1,0:T(8,128)}, u32[]{:S(2)}) copy-start(s32[8,8]{1,0:T(8,128)} %copy-done.8) | copy-start | bytes 772
  69.3 2.0 %copy-start.2 = (f32[4,2,128,1024]{3,2,1,0:T(8,128)}, f32[4,2,128,1024]{3,2,1,0:T(8,128)S(1)}, u32[]{:S(2)}) copy-start(f32[4,2,128,1024]{3,2,1,0:T(8,128)S(1)} %add_returned.2.grad_in_ref) | copy-start | bytes 12582916

commit v3 on v2

--- a/solution.py
+++ b/solution.py
@@ -198,7 +198,7 @@
         own_ref = own_in_ref
         sems, = refs
     else:
-        own_ref, left_ref, sem, sems = refs
+        own_ref, sem, sems = refs
         load = pltpu.make_async_copy(own_in_ref, own_ref, sem)
         load.start()
     width = own_ref.shape[2]
@@ -232,15 +232,9 @@
             told = jnp.where(index == r * width + s, plan_ref[r, s].astype(jnp.float32), told)
     push_ref[push_ref.shape[0] - 1, 0] = told
     if not again:
-        left_ref[...] = jnp.full(left_ref.shape, plan_ref[TOTALS, 2].astype(jnp.float32))
         load.wait()
     lax.fori_loop(0, plan_ref[TOTALS, 0], step, 0)
     lax.fori_loop(0, plan_ref[TOTALS, 0], end, 0)
-
-
-def start_kernel(lefts_ref, plan_ref, grad_ref, left_ref):
-    grad_ref[...] = jnp.zeros_like(grad_ref)
-    left_ref[0] = jnp.sum(lefts_ref[...])
 
 
 def pull_kernel(told_ref, own_ref, plan_ref, pull_ref, whole_ref, numbers_ref, sem):
@@ -261,12 +255,15 @@
     lax.fori_loop(0, plan_ref[TOTALS, 1], step, 0)
 
 
-def grad_kernel(plan_ref, probe_ref, own_ref, came_ref, tables_ref, loss_in_ref, *refs, pushed):
+def grad_kernel(plan_ref, probe_ref, own_ref, came_ref, tables_ref, *refs, pushed):
     if pushed:
-        grad_in_ref, grad_ref, back_ref, loss_ref, wave_ref, window_ref = refs
+        grad_ref, back_ref, loss_ref, wave_ref, window_ref = refs
+        grad_ref[...] = jnp.zeros_like(grad_ref)
+        before = jnp.float32(0.0)
     else:
-        grad_in_ref, seen_ref, grad_ref, back_ref, loss_ref, wave_ref, window_ref = refs
-    grad_ref[...] = grad_in_ref[...]
+        loss_in_ref, grad_in_ref, seen_ref, grad_ref, back_ref, loss_ref, wave_ref, window_ref = refs
+        grad_ref[...] = grad_in_ref[...]
+        before = loss_in_ref[0]
     slices, planes, width, columns = own_ref.shape
     units = width // UNIT
     seen_units = width // (UNIT * UNIT)
@@ -329,11 +326,17 @@
 
         return loss
 
-    loss_ref[0] = lax.fori_loop(0, (count + BATCH - 1) // BATCH, step, loss_in_ref[0])
-
-
-def after_kernel(loss_ref, x_ref, first_ref, x_out_ref, losses_ref):
-    losses_ref[...] = jnp.full(losses_ref.shape, loss_ref[0])
+    loss_ref[0] = lax.fori_loop(0, (count + BATCH - 1) // BATCH, step, before)
+    loss_ref[1] = plan_ref[TOTALS, 2].astype(jnp.float32)
+
+
+def after_kernel(x_ref, *refs):
+    pass
+
+
+def after_last_kernel(x_ref, last_ref, out_ref):
+    for i in range(out_ref.shape[0]):
+        out_ref[i] = x_ref[i]
 
 
 def add(plan, slot, grad_ref, layers, came, start, begin, end, below):
@@ -379,27 +382,52 @@
     lax.fori_loop(0, before_ref[TOTALS, 1], step, 0)
 
 
-def add_given_kernel(before_ref, given_ref, grad_in_ref, grad_ref):
-    grad_ref[...] = grad_in_ref[...]
-    add_given(before_ref, given_ref, grad_ref, range(grad_ref.shape[0]))
-
-
-def finish_kernel(before_ref, given_ref, losses_ref, grad_in_ref, grad_hbm, loss_ref, grad_ref, sems):
+def finish_kernel(before_ref, given_ref, grad_in_ref, grad_hbm, grad_ref, sems):
     slices = grad_ref.shape[0]
     stores = [pltpu.make_async_copy(grad_ref.at[l], grad_hbm.at[l], sems.at[l]) for l in range(slices)]
     for l in range(slices):
         grad_ref[l] = grad_in_ref[l]
         add_given(before_ref, given_ref, grad_ref, [l])
         stores[l].start()
-    lanes = lax.broadcasted_iota(jnp.int32, losses_ref.shape, 1)
-    loss_ref[0] = jnp.sum(jnp.where(lanes == 0, losses_ref[...], 0.0))
     for store in stores:
+        store.wait()
+
+
+def merge_kernel(more_ref, base_hbm, sum_hbm, work_ref, sem):
+    for l in range(work_ref.shape[0]):
+        load = pltpu.make_async_copy(base_hbm.at[l], work_ref.at[l], sem)
+        load.start()
+        load.wait()
+        work_ref[l] += more_ref[l]
+        store = pltpu.make_async_copy(work_ref.at[l], sum_hbm.at[l], sem)
+        store.start()
         store.wait()
 
 
 def shifted(x, axis, by):
     peers = lax.axis_size(axis)
     return lax.ppermute(x, axis, [(i, (i + by) % peers) for i in range(peers)])
+
+
+def total_stages(peers):
+    stages, step = [], 1
+    while step < peers:
+        radix = 4 if step * 4 <= peers else 2
+        stages.append((step, radix))
+        step *= radix
+    return stages
+
+
+def partial_total(x, axis, stage):
+    peers = lax.axis_size(axis)
+    step, radix = stage
+
+    def other(by):
+        return lax.ppermute(x, axis, [(i, i ^ by) for i in range(peers)])
+
+    if radix == 2:
+        return x + other(step)
+    return (x + other(step)) + (other(2 * step) + other(3 * step))
 
 
 def local(probe_wave, object_slices, intensities, row_offset, col_offset, counts):
@@ -439,20 +467,22 @@
     def held(like):
         return pltpu.VMEM(like.shape, like.dtype)
 
-    strip = shape(object_slices.shape)
+    strip, sums_shape = shape(object_slices.shape), shape((2,))
     plan_shape = shape((8, cap), jnp.int32)
-    rows = shape((peers, width))
-    one = shape((1,))
     dma = pltpu.SemaphoreType.DMA
 
-    def ahead(source, again):
+    def held(like):
+        return pltpu.VMEM(like.shape, like.dtype)
+
+    def ahead(meta, source, again):
         kernel = functools.partial(push_kernel, rooms=rooms, again=again)
-        ins, outs = (meta, source, seen), (plan_shape, held(packed(rooms[again][0] + 1)))
+        outs = (plan_shape, held(packed(rooms[again][0] + 1)))
         if again:
-            return call(kernel, "pack_more", 4, ins, [smem, vmem, anywhere], outs, (smem, vmem), [dma((cap,))])
+            return call(kernel, "pack_more", 4, (meta, source, seen), [smem, vmem, anywhere], outs, (smem, vmem), [dma((cap,))])
+        far = [pltpu.with_memory_space_constraint(x, pltpu.HBM) for x in (source, seen)]
         return call(
-            kernel, "pack_pushed", 4, (meta,) + tuple(pltpu.with_memory_space_constraint(x, pltpu.HBM) for x in (source, seen)),
-            [smem, anywhere, anywhere], outs + (held(strip), rows), (smem, vmem, vmem, vmem), [dma, dma((cap,))],
+            kernel, "pack_pushed", 4, (meta, *far), [smem, anywhere, anywhere], outs + (held(strip),), (smem, vmem, vmem),
+            [dma, dma((cap,))],
         )
 
     def behind(pushed, own, again):
@@ -460,60 +490,56 @@
         outs = (plan_shape, held(packed(rooms[again][2])))
         return call(pull_kernel, "pack_pulled", 2, (pushed, own), [vmem, vmem], outs, (smem, vmem), scratch)
 
-    def grads(plan, own, came, loss, grad, back, is_pushed):
-        name, more = ("grads_pushed", ()) if is_pushed else ("grads_kept", (intensities,))
+    def grads(plan, own, came, back, *kept):
         buffer = pltpu.VMEM((BATCH, slices, planes, width, width), f32)
         return call(
-            functools.partial(grad_kernel, pushed=is_pushed), name, 10,
-            (plan, probe_wave, own, came, tables, loss, grad) + more,
-            [smem] + [vmem] * 4 + [smem, vmem] + [vmem] * len(more),
-            (held(strip), held(packed(back)), one), (vmem, vmem, smem), [buffer, buffer], 24, {6: 0},
+            functools.partial(grad_kernel, pushed=not kept), "grads_kept" if kept else "grads_pushed", 10,
+            (plan, probe_wave, own, came, tables, *kept), [smem] + [vmem] * 4 + ([smem, vmem, vmem] if kept else []),
+            (held(strip), held(packed(back)), sums_shape), (vmem, vmem, smem), [buffer, buffer], 24, {6: 0} if kept else {},
         )
 
-    def add_returned(plan, returned, grad):
-        return call(
-            add_returned_kernel, "add_returned", 1, (plan, returned, grad), [smem, vmem, vmem], held(strip), vmem, aliases={2: 0}
+    stages = total_stages(peers)
+
+    def one_round(own, plan, push, again):
+        pushed = shifted(push, "tile", 1)
+        before, pull = behind(pushed, own, again)
+        pulled = shifted(pull, "tile", -1)
+        grad, back, sums = grads(before, own, pushed, rooms[again][1])
+        returned = shifted(back, "tile", -1)
+        grad, back, sums = grads(plan, own, pulled, rooms[again][2], sums, grad, intensities)
+        sums = partial_total(sums, "tile", stages[0])
+        back = call(
+            after_kernel, "after_returned", 1, (back, returned, sums), [anywhere] * 3, held(back), anywhere, aliases={0: 0}
         )
-
-    plan, push, own, left = ahead(object_slices, False)
-    pushed = shifted(push, "tile", 1)
-    lefts = lax.all_to_all(left, "tile", 0, 0, tiled=True)
-    before, pull = behind(pushed, own, False)
-    pulled = shifted(pull, "tile", -1)
-    grad, left = call(start_kernel, "start", 1, (lefts, before), [vmem, smem], (held(strip), one), (vmem, smem))
+        given = shifted(back, "tile", 1)
+        grad = call(
+            add_returned_kernel, "add_returned", 1, (plan, returned, grad), [smem, vmem, vmem], held(strip), vmem,
+            aliases={2: 0},
+        )
+        sums = call(after_last_kernel, "after_given", 1, (sums, given), [smem, anywhere], sums_shape, smem)
+        for stage in stages[1:]:
+            sums = partial_total(sums, "tile", stage)
+        grad = call(
+            finish_kernel, "add_given", 4, (before, given, grad), [smem, vmem, vmem], pltpu.HBM(strip.shape, f32), anywhere,
+            [pltpu.VMEM(strip.shape, f32), dma((slices,))],
+        )
+        return grad, sums
 
     def unfinished(carry):
-        return carry[2][0] > 0
+        return carry[1][1] > 0
 
     def second(carry):
-        grad, loss, _ = carry
-        plan, push = ahead(own, True)
-        pushed = shifted(push, "tile", 1)
-        before, pull = behind(pushed, own, True)
-        pulled = shifted(pull, "tile", -1)
-        grad, back, loss = grads(before, own, pushed, loss, grad, rooms[1][1], True)
-        returned = shifted(back, "tile", -1)
-        grad, back, loss = grads(plan, own, pulled, loss, grad, rooms[1][2], False)
-        given = shifted(back, "tile", 1)
-        grad = add_returned(plan, returned, grad)
-        grad = call(add_given_kernel, "add_given", 1, (before, given, grad), [smem, vmem, vmem], held(strip), vmem, aliases={2: 0})
-        return grad, loss, jnp.zeros_like(left)
-
-    grad, loss, _ = lax.while_loop(unfinished, second, (grad, jnp.zeros((1,), f32), left))
-    grad, back, loss = grads(before, own, pushed, loss, grad, rooms[0][1], True)
-    returned = shifted(back, "tile", -1)
-    grad, back, loss = grads(plan, own, pulled, loss, grad, rooms[0][2], False)
-    back, losses = call(
-        after_kernel, "after_returned", 1, (loss, back, returned), [smem, anywhere, anywhere],
-        (held(back), rows), (anywhere, vmem), aliases={1: 0},
-    )
-    given = shifted(back, "tile", 1)
-    losses = lax.all_to_all(losses, "tile", 0, 0, tiled=True)
-    grad = add_returned(plan, returned, grad)
-    return call(
-        finish_kernel, "add_given", 4, (before, given, losses, grad), [smem, vmem, vmem, vmem],
-        (strip, one), (anywhere, smem), [pltpu.VMEM(strip.shape, f32), dma((slices,))],
-    )
+        grad, sums, meta = carry
+        more, more_sums = one_round(own, *ahead(meta, own, True), True)
+        grad = call(
+            merge_kernel, "merge", 4, (more, pltpu.with_memory_space_constraint(grad, pltpu.HBM)), [vmem, anywhere],
+            pltpu.HBM(strip.shape, f32), anywhere, [pltpu.VMEM(strip.shape, f32), dma], aliases={1: 0},
+        )
+        return grad, jnp.stack([sums[0] + more_sums[0], jnp.float32(0.0)]), jnp.zeros_like(meta)
+
+    plan, push, own = ahead(meta, object_slices, False)
+    grad, sums, _ = lax.while_loop(unfinished, second, (*one_round(own, plan, push, False), meta))
+    return grad, sums[:1]
 
 
 def solution(mesh):

time: 82.6 us -> 84.9 us (1.028); the launches traced: 81.9 us -> 85.4 us
  waiting for transfers between devices: 22.9 us -> 41.1 us
  Pallas kernels: 32.2 us -> 22.7 us
  local copies, waits for them, and re-layouts: 8.46 us -> 1.33 us
  starting transfers between devices: 15 us -> 16.9 us
    ppermute x4, waiting for transfers between devices: 17.9 us -> 37.9 us  [shifted(): return lax.ppermute(x, axis, [(i, (i + by) % peers) for i in range(peers)])]
    ppermute x0 -> x6, starting transfers between devices: none -> 15.2 us  [other(): return lax.ppermute(x, axis, [(i, i ^ by) for i in range(peers)])]
    all_to_all x2 -> x0, starting transfers between devices: 12.1 us -> none  [the longest x1 6.85 us: local(): lefts = lax.all_to_all(left, 'tile', 0, 0, tiled=True)]
    pallas_call x8, Pallas kernels: 32.2 us -> 22.7 us  [call(): pl.pallas_call(kernel, out_shape=outs, in_specs=in_specs, out_specs=out_s...]
    unnamed x20 -> x8, local copies, waits for them, and re-layouts: 8.46 us -> 0.03 us
    all_to_all x2 -> x0, waiting for transfers between devices: 4.98 us -> none  [the longest x1 4.98 us: local(): losses = lax.all_to_all(losses, 'tile', 0, 0, tiled=True)]
    ppermute x0 -> x6, waiting for transfers between devices: none -> 3.19 us  [other(): return lax.ppermute(x, axis, [(i, i ^ by) for i in range(peers)])]
    slice x0 -> x1, local copies, waits for them, and re-layouts: none -> 1.3 us  [unfinished(): return carry[1][1] > 0]
  transfers between devices with their start and end apart: 6 -> 10, of which waited for: 3 -> 6; matrix products, arithmetic and copies ran while one was open for 0% -> 0% of each run, Pallas kernels for 26% -> 19%
where the time goes in v3:
time: 84.9 us; the launch traced here: 85.4 us
  waiting for transfers between devices  41.1 us (48%)
  Pallas kernels  22.7 us (27%)
  starting transfers between devices  16.9 us (20%)
  between operations  1.6 us (2%)
  local copies, waits for them, and re-layouts  1.33 us (2%)
  other arithmetic  1.27 us (1%)
    ppermute x4, waiting for transfers between devices, shifted(): return lax.ppermute(x, axis, [(i, (i + by) % peers) for i in range(peers)])  37.9 us
    pallas_call x8, Pallas kernels, call(): pl.pallas_call(kernel, out_shape=outs, in_specs=in_specs, out_specs=out_s...  22.7 us
    ppermute x6, starting transfers between devices, other(): return lax.ppermute(x, axis, [(i, i ^ by) for i in range(peers)])  15.2 us
    ppermute x6, waiting for transfers between devices, other(): return lax.ppermute(x, axis, [(i, i ^ by) for i in range(peers)])  3.19 us
    ppermute x4, starting transfers between devices, shifted(): return lax.ppermute(x, axis, [(i, (i + by) % peers) for i in range(peers)])  1.7 us
  transfers between devices with their start and end apart: 10, of which 6 were waited for; matrix products, arithmetic and copies ran while one was open for 0% of the time, Pallas kernels for 19%

profile of v3, /device:TPU:0, one launch (start us, length us, event | category | flops | bytes accessed | tf_op | source)
XLA Modules:
  0.0 85.4 jit_solution(6071454736203700841)
XLA Ops:
  1.3 0.7 pad_add_fusion.meta_ref
  2.0 3.7 %pack_pushed.1 = (s32[8,8]{1,0:T(8,128)S(1)}, f32[37,8,8,128]{3,2,1,0:T(8,128)S(1)}, f32[4,2,128,1024]{3,2,1,0:T(8,128)S(1)}) custom-call(s32[17]{0:T(128)S(1)} %pad_add_fusion.meta_ref, f32[4,2,128,1024]{3,2,1,0:T(8,128)} %own_in_ref.1, f32[8,2,8,8,128]{4,3,2,1,0:T(8,128)} %bitcast.11), custom_call_target="tpu_custom_call" | custom-call | flops 4000000000 | bytes 4000000 | tf_op jit(solution)/shard_map/pack_pushed/pallas_call | solution.py:455
  5.8 0.0 copy-start
  5.8 0.0 copy-start.3
  5.8 0.3 collective-permute-start.10
  6.1 19.7 %collective-permute-done.10.told_ref.came_ref = f32[37,8,8,128]{3,2,1,0:T(8,128)S(1)} collective-permute-done((f32[37,8,8,128]{3,2,1,0:T(8,128)S(1)}, f32[37,8,8,128]{3,2,1,0:T(8,128)S(1)}, u32[]{:S(2)}, u32[]{:S(2)}) %collective-permute-start.10) | collective-permute-done | bytes 1212448 | tf_op jit(solution)/shard_map/ppermute | solution.py:409
  25.8 1.8 %pack_pulled.2 = (s32[8,8]{1,0:T(8,128)S(1)}, f32[33,8,8,128]{3,2,1,0:T(8,128)S(1)}) custom-call(f32[37,8,8,128]{3,2,1,0:T(8,128)S(1)} %collective-permute-done.10.told_ref.came_ref, f32[4,2,128,1024]{3,2,1,0:T(8,128)S(1)} %get-tuple-element.203.own_ref), custom_call_target="tpu_custom_call" | custom-call | flops 2000000000 | bytes 2000000 | tf_op jit(solution)/shard_map/pack_pulled/pallas_call | solution.py:455
  27.6 0.1 collective-permute-start.11
  27.6 0.0 copy-start.2
  27.7 8.7 %grads_pushed.2 = (f32[4,2,128,1024]{3,2,1,0:T(8,128)S(1)}, f32[27,8,8,128]{3,2,1,0:T(8,128)S(1)}, f32[2]{0:T(128)S(1)}) custom-call(s32[8,8]{1,0:T(8,128)S(1)} %get-tuple-element.68.plan_ref.before_ref, f32[2,128,128]{2,1,0:T(8,128)S(1)} %copy-done.3, f32[4,2,128,1024]{3,2,1,0:T(8,128)S(1)} %get-tuple-element.203.own_ref, ...), custom_call_target="tpu_custom_call" | custom-call | flops 10000000000 | bytes 10000000 | tf_op jit(solution)/shard_map/grads_pushed/pallas_call | solution.py:455
  36.4 1.3 %collective-permute-start.12 = (f32[27,8,8,128]{3,2,1,0:T(8,128)S(1)}, f32[27,8,8,128]{3,2,1,0:T(8,128)S(1)}, u32[]{:S(2)}, u32[]{:S(2)}) collective-permute-start(f32[27,8,8,128]{3,2,1,0:T(8,128)S(1)} %get-tuple-element.74), channel_id=1, source_target_pairs={{0,15},{1,0},{2,1},{3,2},{4,3},{5,4},{6,5},{7,6},{8,7},{9,8},{10,9... | collective-permute-start | bytes 2654216 | tf_op jit(solution)/shard_map/ppermute | solution.py:409
  37.7 2.6 %collective-permute-done.11.came_ref = f32[33,8,8,128]{3,2,1,0:T(8,128)S(1)} collective-permute-done((f32[33,8,8,128]{3,2,1,0:T(8,128)S(1)}, f32[33,8,8,128]{3,2,1,0:T(8,128)S(1)}, u32[]{:S(2)}, u32[]{:S(2)}) %collective-permute-start.11) | collective-permute-done | bytes 1081376 | tf_op jit(solution)/shard_map/ppermute | solution.py:409
  40.3 1.9 %grads_kept.2 = (f32[4,2,128,1024]{3,2,1,0:T(8,128)S(1)}, f32[33,8,8,128]{3,2,1,0:T(8,128)S(1)}, f32[2]{0:T(128)S(1)}) custom-call(s32[8,8]{1,0:T(8,128)S(1)} %get-tuple-element.69.plan_ref, f32[2,128,128]{2,1,0:T(8,128)S(1)} %copy-done.3, f32[4,2,128,1024]{3,2,1,0:T(8,128)S(1)} %get-tuple-element.203.own_ref, ...), custom_call_target="tpu_custom_call", output_to_operand_aliasing={{0}: (6, {})} | custom-call | flops 10000000000 | bytes 10000000 | tf_op jit(solution)/shard_map/grads_kept/pallas_call | solution.py:455
  42.2 6.1 %collective-permute-start.13 = (f32[2]{0:T(128)S(1)}, f32[2]{0:T(128)S(1)}, u32[]{:S(2)}, u32[]{:S(2)}) collective-permute-start(f32[2]{0:T(128)S(1)} %get-tuple-element.75), channel_id=1, source_target_pairs={{0,1},{1,0},{2,3},{3,2},{4,5},{5,4},{6,7},{7,6},{8,9},{9,8},{10,11... | collective-permute-start | bytes 32 | tf_op jit(solution)/shard_map/ppermute | solution.py:426
  48.3 3.3 %collective-permute-start.14 = (f32[2]{0:T(128)S(1)}, f32[2]{0:T(128)S(1)}, u32[]{:S(2)}, u32[]{:S(2)}) collective-permute-start(f32[2]{0:T(128)S(1)} %get-tuple-element.75), channel_id=1, source_target_pairs={{0,2},{1,3},{2,0},{3,1},{4,6},{5,7},{6,4},{7,5},{8,10},{9,11},{10,... | collective-permute-start | bytes 32 | tf_op jit(solution)/shard_map/ppermute | solution.py:426
  51.5 0.0 collective-permute-start.15
  51.5 0.0 collective-permute-done.13
  51.5 1.5 %collective-permute-done.14 = f32[2]{0:T(128)S(1)} collective-permute-done((f32[2]{0:T(128)S(1)}, f32[2]{0:T(128)S(1)}, u32[]{:S(2)}, u32[]{:S(2)}) %collective-permute-start.14) | collective-permute-done | bytes 40 | tf_op jit(solution)/shard_map/ppermute | solution.py:426
  53.1 1.4 %collective-permute-done.15 = f32[2]{0:T(128)S(1)} collective-permute-done((f32[2]{0:T(128)S(1)}, f32[2]{0:T(128)S(1)}, u32[]{:S(2)}, u32[]{:S(2)}) %collective-permute-start.15) | collective-permute-done | bytes 40 | tf_op jit(solution)/shard_map/ppermute | solution.py:426
  54.5 0.1 collective-permute-start.16
  54.6 1.6 %add_returned.2.grad_in_ref = f32[4,2,128,1024]{3,2,1,0:T(8,128)S(1)} custom-call(s32[8,8]{1,0:T(8,128)S(1)} %get-tuple-element.69.plan_ref, f32[27,8,8,128]{3,2,1,0:T(8,128)S(1)} %collective-permute-done.12.refs_0_.returned_ref, f32[4,2,128,1024]{3,2,1,0:T(8,128)S(1)} %get-tuple-element.76.grad_in_ref), custom_call_target="tpu_custom_call", output_to_operand_aliasing={{}: (2, {})} | custom-call | flops 1000000000 | bytes 1000000 | tf_op jit(solution)/shard_map/add_returned/pallas_call | solution.py:455
  56.2 15.6 %collective-permute-done.16.given_ref.last_ref = f32[33,8,8,128]{3,2,1,0:T(8,128)S(1)} collective-permute-done((f32[33,8,8,128]{3,2,1,0:T(8,128)S(1)}, f32[33,8,8,128]{3,2,1,0:T(8,128)S(1)}, u32[]{:S(2)}, u32[]{:S(2)}) %collective-permute-start.16) | collective-permute-done | bytes 1081376 | tf_op jit(solution)/shard_map/ppermute | solution.py:409
  71.9 1.1 %after_given.2 = f32[2]{0:T(128)S(1)} custom-call(f32[2]{0:T(128)S(1)} %add_add_fusion.3.refs_1_.x_ref, f32[33,8,8,128]{3,2,1,0:T(8,128)S(1)} %collective-permute-done.16.given_ref.last_ref), custom_call_target="tpu_custom_call" | custom-call | flops 1000000000 | bytes 1000000 | tf_op jit(solution)/shard_map/after_given/pallas_call | solution.py:455
  73.0 0.0 copy-start.4
  73.0 0.1 collective-permute-start.17
  73.1 4.4 %collective-permute-start.18 = (f32[2]{0:T(128)S(1)}, f32[2]{0:T(128)S(1)}, u32[]{:S(2)}, u32[]{:S(2)}) collective-permute-start(f32[2]{0:T(128)S(1)} %after_given.2), channel_id=1, source_target_pairs={{0,8},{1,9},{2,10},{3,11},{4,12},{5,13},{6,14},{7,15},{8,0},{9,1},... | collective-permute-start | bytes 32 | tf_op jit(solution)/shard_map/ppermute | solution.py:426
  77.5 1.4 %collective-permute-start.19 = (f32[2]{0:T(128)S(1)}, f32[2]{0:T(128)S(1)}, u32[]{:S(2)}, u32[]{:S(2)}) collective-permute-start(f32[2]{0:T(128)S(1)} %after_given.2), channel_id=1, source_target_pairs={{0,12},{1,13},{2,14},{3,15},{4,8},{5,9},{6,10},{7,11},{8,4},{9,5},... | collective-permute-start | bytes 32 | tf_op jit(solution)/shard_map/ppermute | solution.py:426
  78.9 3.7 %add_given.2 = f32[4,2,128,1024]{3,2,1,0:T(8,128)} custom-call(s32[8,8]{1,0:T(8,128)S(1)} %get-tuple-element.68.plan_ref.before_ref, f32[33,8,8,128]{3,2,1,0:T(8,128)S(1)} %collective-permute-done.16.given_ref.last_ref, f32[4,2,128,1024]{3,2,1,0:T(8,128)S(1)} %add_returned.2.grad_in_ref), custom_call_target="tpu_custom_call" | custom-call | flops 4000000000 | bytes 4000000 | tf_op jit(solution)/shard_map/add_given/pallas_call | solution.py:455
  82.6 0.2 collective-permute-done.19
  82.8 0.5 add_add_fusion.2
  83.3 1.9 %while.13 = (f32[4,2,128,1024]{3,2,1,0:T(8,128)}, f32[2]{0:T(128)}, s32[17]{0:T(128)S(1)}, f32[4,2,128,1024]{3,2,1,0:T(8,128)S(1)}, f32[8,2,8,8,128]{4,3,2,1,0:T...) while((f32[4,2,128,1024]{3,2,1,0:T(8,128)}, f32[2]{0:T(128)}, ...), condition=%wide.region_1.0_spmd.clone, body=%wide.region_0.0_spmd.sunk.clone.sunk | while | flops 36999999488 | bytes 73832136 | solution.py:541
  83.3 1.3 %slice.18 = f32[1]{0:T(128)} slice(f32[2]{0:T(128)} %get-tuple-element.144), slice={[1:2]} | slice | bytes 8 | tf_op jit(solution)/shard_map/while/cond/slice | solution.py:529
  (9 shorter events, 0.0 us)
Async XLA Ops:
  5.8 21.8 %copy-start = (bf16[2,2,2,256,256]{4,3,2,1,0:T(8,128)(2,1)S(1)}, bf16[2,2,2,256,256]{4,3,2,1,0:T(8,128)(2,1)}, u32[]{:S(2)}) copy-start(bf16[2,2,2,256,256]{4,3,2,1,0:T(8,128)(2,1)} %constant.9.clone.tables_ref) | copy-start | bytes 3145732
  5.8 21.8 %copy-start.3 = (f32[2,128,128]{2,1,0:T(8,128)S(1)}, f32[2,128,128]{2,1,0:T(8,128)}, u32[]{:S(2)}) copy-start(f32[2,128,128]{2,1,0:T(8,128)} %probe_ref.3) | copy-start | bytes 393220
  5.8 20.0 %collective-permute-start.10 = (f32[37,8,8,128]{3,2,1,0:T(8,128)S(1)}, f32[37,8,8,128]{3,2,1,0:T(8,128)S(1)}, u32[]{:S(2)}, u32[]{:S(2)}) collective-permute-start(f32[37,8,8,128]{3,2,1,0:T(8,128)S(1)} %get-tuple-element.66), channel_id=1, source_target_pairs={{0,1},{1,2},{2,3},{3,4},{4,5},{5,6},{6,7},{7,8},{8,9},{9,10},{10,1... | collective-permute-start | bytes 3637256 | tf_op jit(solution)/shard_map/ppermute | solution.py:409
  27.6 12.7 %collective-permute-start.11 = (f32[33,8,8,128]{3,2,1,0:T(8,128)S(1)}, f32[33,8,8,128]{3,2,1,0:T(8,128)S(1)}, u32[]{:S(2)}, u32[]{:S(2)}) collective-permute-start(f32[33,8,8,128]{3,2,1,0:T(8,128)S(1)} %get-tuple-element.70), channel_id=1, source_target_pairs={{0,15},{1,0},{2,1},{3,2},{4,3},{5,4},{6,5},{7,6},{8,7},{9,8},{10,9... | collective-permute-start | bytes 3244040 | tf_op jit(solution)/shard_map/ppermute | solution.py:409
  27.6 12.6 %copy-start.2 = (f32[8,128,128]{2,1,0:T(8,128)S(1)}, f32[8,128,128]{2,1,0:T(8,128)}, u32[]{:S(2)}) copy-start(f32[8,128,128]{2,1,0:T(8,128)} %refs_2_.1) | copy-start | bytes 1572868
  36.4 18.1 %collective-permute-start.12 = (f32[27,8,8,128]{3,2,1,0:T(8,128)S(1)}, f32[27,8,8,128]{3,2,1,0:T(8,128)S(1)}, u32[]{:S(2)}, u32[]{:S(2)}) collective-permute-start(f32[27,8,8,128]{3,2,1,0:T(8,128)S(1)} %get-tuple-element.74), channel_id=1, source_target_pairs={{0,15},{1,0},{2,1},{3,2},{4,3},{5,4},{6,5},{7,6},{8,7},{9,8},{10,9... | collective-permute-start | bytes 2654216 | tf_op jit(solution)/shard_map/ppermute | solution.py:409
  42.2 9.3 %collective-permute-start.13 = (f32[2]{0:T(128)S(1)}, f32[2]{0:T(128)S(1)}, u32[]{:S(2)}, u32[]{:S(2)}) collective-permute-start(f32[2]{0:T(128)S(1)} %get-tuple-element.75), channel_id=1, source_target_pairs={{0,1},{1,0},{2,3},{3,2},{4,5},{5,4},{6,7},{7,6},{8,9},{9,8},{10,11... | collective-permute-start | bytes 32 | tf_op jit(solution)/shard_map/ppermute | solution.py:426
  48.3 4.8 %collective-permute-start.14 = (f32[2]{0:T(128)S(1)}, f32[2]{0:T(128)S(1)}, u32[]{:S(2)}, u32[]{:S(2)}) collective-permute-start(f32[2]{0:T(128)S(1)} %get-tuple-element.75), channel_id=1, source_target_pairs={{0,2},{1,3},{2,0},{3,1},{4,6},{5,7},{6,4},{7,5},{8,10},{9,11},{10,... | collective-permute-start | bytes 32 | tf_op jit(solution)/shard_map/ppermute | solution.py:426
  51.5 3.0 %collective-permute-start.15 = (f32[2]{0:T(128)S(1)}, f32[2]{0:T(128)S(1)}, u32[]{:S(2)}, u32[]{:S(2)}) collective-permute-start(f32[2]{0:T(128)S(1)} %get-tuple-element.75), channel_id=1, source_target_pairs={{0,3},{1,2},{2,1},{3,0},{4,7},{5,6},{6,5},{7,4},{8,11},{9,10},{10,... | collective-permute-start | bytes 32 | tf_op jit(solution)/shard_map/ppermute | solution.py:426
  54.5 17.3 %collective-permute-start.16 = (f32[33,8,8,128]{3,2,1,0:T(8,128)S(1)}, f32[33,8,8,128]{3,2,1,0:T(8,128)S(1)}, u32[]{:S(2)}, u32[]{:S(2)}) collective-permute-start(f32[33,8,8,128]{3,2,1,0:T(8,128)S(1)} %after_returned.2), channel_id=1, source_target_pairs={{0,1},{1,2},{2,3},{3,4},{4,5},{5,6},{6,7},{7,8},{8,9},{9,10},{10,1... | collective-permute-start | bytes 3244040 | tf_op jit(solution)/shard_map/ppermute | solution.py:409
  73.0 10.3 %copy-start.4 = (bf16[2,2,2,256,256]{4,3,2,1,0:T(8,128)(2,1)S(1)}, bf16[2,2,2,256,256]{4,3,2,1,0:T(8,128)(2,1)}, u32[]{:S(2)}) copy-start(bf16[2,2,2,256,256]{4,3,2,1,0:T(8,128)(2,1)} %constant.9.clone..sunk.2) | copy-start | bytes 3145732
  73.0 9.6 %collective-permute-start.17 = (f32[2]{0:T(128)S(1)}, f32[2]{0:T(128)S(1)}, u32[]{:S(2)}, u32[]{:S(2)}) collective-permute-start(f32[2]{0:T(128)S(1)} %after_given.2), channel_id=1, source_target_pairs={{0,4},{1,5},{2,6},{3,7},{4,0},{5,1},{6,2},{7,3},{8,12},{9,13},{10,... | collective-permute-start | bytes 32 | tf_op jit(solution)/shard_map/ppermute | solution.py:426
  73.1 9.5 %collective-permute-start.18 = (f32[2]{0:T(128)S(1)}, f32[2]{0:T(128)S(1)}, u32[]{:S(2)}, u32[]{:S(2)}) collective-permute-start(f32[2]{0:T(128)S(1)} %after_given.2), channel_id=1, source_target_pairs={{0,8},{1,9},{2,10},{3,11},{4,12},{5,13},{6,14},{7,15},{8,0},{9,1},... | collective-permute-start | bytes 32 | tf_op jit(solution)/shard_map/ppermute | solution.py:426
  77.5 5.3 %collective-permute-start.19 = (f32[2]{0:T(128)S(1)}, f32[2]{0:T(128)S(1)}, u32[]{:S(2)}, u32[]{:S(2)}) collective-permute-start(f32[2]{0:T(128)S(1)} %after_given.2), channel_id=1, source_target_pairs={{0,12},{1,13},{2,14},{3,15},{4,8},{5,9},{6,10},{7,11},{8,4},{9,5},... | collective-permute-start | bytes 32 | tf_op jit(solution)/shard_map/ppermute | solution.py:426
